TPU v7x, 32 devices: a whole 2x2x4 slice. The times are simulated.
32 devices in a mesh: dp: 8 (over z, y), seq: 4 (over x, core).
Axes of the slice: x: 2, y: 2, z: 4, core: 2. Of those that a mesh axis runs over, the one named last changes fastest.
Arguments:
- activations: bfloat16 [8, 1280, 512], P('dp', 'seq'), may hold values from -6 to 6
- encoder_attention_norm_gain: bfloat16 [512], P('seq'), may hold values from 0.5 to 1.5
- encoder_attention_norm_bias: bfloat16 [512], P('seq'), may hold values from -3 to 3
- encoder_query_key_value_weight: bfloat16 [512, 1536], P('seq'), may hold values from -0.25 to 0.25
- encoder_attention_output_weight: bfloat16 [512, 512], P('seq'), may hold values from -1 to 1
- encoder_attention_layer_scale: bfloat16 [512], P('seq'), may hold values from 0.5 to 1.5
- encoder_forward_norm_gain: bfloat16 [512], P('seq'), may hold values from 0.5 to 1.5
- encoder_forward_norm_bias: bfloat16 [512], P('seq'), may hold values from -3 to 3
- encoder_forward_input_weight: bfloat16 [512, 2048], P('seq'), may hold values from -0.25 to 0.25
- encoder_forward_output_weight: bfloat16 [2048, 512], P('seq'), may hold values from -0.125 to 0.125
- encoder_forward_layer_scale: bfloat16 [512], P('seq'), may hold values from 0.5 to 1.5
- strided_convolution_weight: bfloat16 [4, 512, 512], P(None, 'seq'), may hold values from -0.125 to 0.125
- strided_convolution_bias: bfloat16 [512], P('seq'), may hold values from -3 to 3
- quantizer_input_weight: bfloat16 [512, 256], P('seq'), may hold values from -0.25 to 0.25
- codebook: bfloat16 [8, 2048, 256], P(None, 'seq'), may hold values from -1.796875 to 1.796875
- quantizer_output_weight: bfloat16 [256, 512], P(None, 'seq'), may hold values from -0.375 to 0.375
- transposed_convolution_weight: bfloat16 [4, 512, 512], P(None, 'seq'), may hold values from -0.1875 to 0.1875
- transposed_convolution_bias: bfloat16 [512], P('seq'), may hold values from -3 to 3
- decoder_attention_norm_gain: bfloat16 [512], P('seq'), may hold values from 0.5 to 1.5
- decoder_attention_norm_bias: bfloat16 [512], P('seq'), may hold values from -3 to 3
- decoder_query_key_value_weight: bfloat16 [512, 1536], P('seq'), may hold values from -0.25 to 0.25
- decoder_attention_output_weight: bfloat16 [512, 512], P('seq'), may hold values from -1 to 1
- decoder_attention_layer_scale: bfloat16 [512], P('seq'), may hold values from 0.5 to 1.5
- decoder_forward_norm_gain: bfloat16 [512], P('seq'), may hold values from 0.5 to 1.5
- decoder_forward_norm_bias: bfloat16 [512], P('seq'), may hold values from -3 to 3
- decoder_forward_input_weight: bfloat16 [512, 2048], P('seq'), may hold values from -0.25 to 0.25
- decoder_forward_output_weight: bfloat16 [2048, 512], P('seq'), may hold values from -0.125 to 0.125
- decoder_forward_layer_scale: bfloat16 [512], P('seq'), may hold values from 0.5 to 1.5
- cotangent: bfloat16 [8, 1280, 512], P('dp', 'seq'), may hold values from -6 to 6
- frame_segment_index: int32 [8, 1280], P('dp'), may hold values from 0 to 1, as said below
- frame_code_index: int32 [8, 640, 8], P('dp', 'seq'), may hold values from 0 to 2047
- replace_code_mask: int32 [8, 2048], replicated, may hold values 0 or 1
- replacing_batch_position: int32 [8, 2048], replicated, may hold values from 0 to 5119
- code_usage_average: float32 [8, 2048], P(None, ('dp', 'seq')), may hold values from 0.25 to 2
- code_latent_sum_average: float32 [8, 2048, 256], P(None, ('dp', 'seq')), may hold values from -6 to 6
Outputs:
- output: bfloat16 [8, 1280, 512], P('dp', 'seq')
- activations_grad: bfloat16 [8, 1280, 512], P('dp', 'seq')
- grad_encoder_gain_one: float32 [512], P(('dp', 'seq'))
- grad_encoder_bias_one: float32 [512], P(('dp', 'seq'))
- grad_encoder_in_proj: float32 [512, 1536], P(('dp', 'seq'))
- grad_encoder_out_proj: float32 [512, 512], P(('dp', 'seq'))
- grad_encoder_scale_one: float32 [512], P(('dp', 'seq'))
- grad_encoder_gain_two: float32 [512], P(('dp', 'seq'))
- grad_encoder_bias_two: float32 [512], P(('dp', 'seq'))
- grad_encoder_linear_one: float32 [512, 2048], P(('dp', 'seq'))
- grad_encoder_linear_two: float32 [2048, 512], P(('dp', 'seq'))
- grad_encoder_scale_two: float32 [512], P(('dp', 'seq'))
- grad_downsample_weight: float32 [4, 512, 512], P(None, ('dp', 'seq'))
- grad_downsample_bias: float32 [512], P(('dp', 'seq'))
- grad_latent_in: float32 [512, 256], P(('dp', 'seq'))
- grad_latent_out: float32 [256, 512], P(None, ('dp', 'seq'))
- grad_upsample_weight: float32 [4, 512, 512], P(None, ('dp', 'seq'))
- grad_upsample_bias: float32 [512], P(('dp', 'seq'))
- grad_decoder_gain_one: float32 [512], P(('dp', 'seq'))
- grad_decoder_bias_one: float32 [512], P(('dp', 'seq'))
- grad_decoder_in_proj: float32 [512, 1536], P(('dp', 'seq'))
- grad_decoder_out_proj: float32 [512, 512], P(('dp', 'seq'))
- grad_decoder_scale_one: float32 [512], P(('dp', 'seq'))
- grad_decoder_gain_two: float32 [512], P(('dp', 'seq'))
- grad_decoder_bias_two: float32 [512], P(('dp', 'seq'))
- grad_decoder_linear_one: float32 [512, 2048], P(('dp', 'seq'))
- grad_decoder_linear_two: float32 [2048, 512], P(('dp', 'seq'))
- grad_decoder_scale_two: float32 [512], P(('dp', 'seq'))
- new_cluster_size: float32 [8, 2048], P(None, ('dp', 'seq'))
- new_embed_sum: float32 [8, 2048, 256], P(None, ('dp', 'seq'))
- new_codebook: float32 [8, 2048, 256], P(None, ('dp', 'seq'))
Inputs may be any that keep to these rules, and one draw needn't show every extreme that they name: `frame_segment_index`: each row is segment 0 up to some frame after its first and segment 1 from that frame on; in each aligned block of 1 row one row turns to segment 1 within its first 160 frames. `replacing_batch_position`: a flat position row * 640 + frame in the whole batch.
All inputs are finite; a program needn't handle non-finite values.
Results may differ from a plain program's by a relative error of at most 0.024.
Values may be sent and summed in bfloat16 or wider, within the bound.
No kernel may reach another device: no remote copies, remote signals or barrier semaphores. Data moves between devices by JAX's collectives and lax.ppermute only.
A program may use at most 256 MiB of HBM per device.

v0:
```python
from functools import partial

import jax
import jax.numpy as jnp
from jax import lax
from jax.experimental import pallas as pl
from jax.experimental.pallas import tpu as pltpu
from jax.sharding import PartitionSpec as P

HEADS = 8
HEAD_DIM = 64
CONTEXT = 250
HALO = 256
CODE_HALO = HALO // 2 + 16
EXTRA = 16
QUERIES = 64
GROUP = 4
WINDOW = HALO + QUERIES
VMEM_LIMIT = 26 * 1024 * 1024
ORDER_A = ("lo", "x", "hi")
ORDER_B = ("lo", "x", "hi")
ORDER_C_ONE = ("x", "lo", "hi")
ORDER_C_TWO = ("lo", "x", "hi")
ORDER_D = ("lo", "x", "hi")
DP = ("hi", "lo")
SEQ = ("x", "core")

norm_eps = 1e-05
ema_decay = 0.9
bf16 = jnp.bfloat16
f32 = jnp.float32


PIECES = 4


def fetch(sc_ref, pieces, at, width, dst, sems, first=0):
    copies = []
    for i, piece in enumerate(pieces):
        rows = piece.shape[0]
        row = pl.multiple_of(sc_ref[8 + i], 128)
        copies.append(
            pltpu.make_async_copy(
                piece.at[:, at : at + width], dst.at[pl.ds(row, rows), :], sems.at[first + i]
            )
        )
        copies[-1].start()
    return copies


def split_refs(refs, counts):
    groups = []
    for count in counts:
        groups.append(refs[:count])
        refs = refs[count:]
    return groups, refs


def wait_all(copies):
    for copy in copies:
        copy.wait()


def mm(a, b):
    return jnp.dot(a, b, preferred_element_type=f32)


def mm_nt(a, b):
    return lax.dot_general(a, b, (((1,), (1,)), ((), ())), preferred_element_type=f32)


def mm_tn(a, b):
    return lax.dot_general(a, b, (((0,), (0,)), ((), ())), preferred_element_type=f32)


def normalize(stream):
    center = stream - jnp.mean(stream, -1, keepdims=True)
    scaled = lax.rsqrt(jnp.mean(center * center, -1, keepdims=True) + norm_eps)
    return center * scaled, scaled


def norm_backward(upstream, normal, scaled, gain):
    inner = upstream * gain
    return scaled * (
        inner
        - jnp.mean(inner, -1, keepdims=True)
        - normal * jnp.mean(inner * normal, -1, keepdims=True)
    )


def column_sum(value):
    return jnp.sum(value, 0, keepdims=True)


def interleave(even, odd, scr):
    tiles, rows, _ = scr.shape
    for tile in range(tiles):
        cols = slice(tile * 128, (tile + 1) * 128)
        scr[tile, pl.ds(0, rows // 2, stride=2), :] = even[:, cols]
        scr[tile, pl.ds(1, rows // 2, stride=2), :] = odd[:, cols]
    return jnp.concatenate([scr[tile] for tile in range(tiles)], 1)


def split_rows(value, scr):
    tiles, rows, _ = scr.shape
    for tile in range(tiles):
        scr[tile] = value[:, tile * 128 : (tile + 1) * 128]
    even = [scr[tile, pl.ds(0, rows // 2, stride=2), :] for tile in range(tiles)]
    odd = [scr[tile, pl.ds(1, rows // 2, stride=2), :] for tile in range(tiles)]
    return jnp.concatenate(even, 1), jnp.concatenate(odd, 1)


def first_half():
    lane = lax.broadcasted_iota(jnp.int32, (1, 128), 1)
    return lane % HEAD_DIM < HEAD_DIM // 2


def rotate(tile, cos, sin):
    swapped = jnp.where(first_half(), pltpu.roll(tile, 96, 1), pltpu.roll(tile, 32, 1))
    return tile * cos + swapped * sin


def head_lanes():
    lane = lax.broadcasted_iota(jnp.int32, (1, GROUP * HEAD_DIM), 1) // HEAD_DIM
    return [(lane == head) for head in range(GROUP)]


def stack_heads(block, lanes):
    return jnp.concatenate([block * mask.astype(bf16) for mask in lanes], 0)


def unstack_heads(block, lanes):
    rows = block.shape[0] // GROUP
    out = block[:rows]
    for head in range(1, GROUP):
        out = jnp.where(lanes[head], block[head * rows : (head + 1) * rows], out)
    return out


def lowest_key(query, cut):
    low = jnp.maximum(query - (CONTEXT - 1), 0)
    return jnp.where(query >= cut, jnp.maximum(low, cut), low)


def attend(q_ref, k_ref, v_ref, att_ref, sc_ref, rows, first_query, first_key, keys, at_row):
    start, cut = sc_ref[0], sc_ref[1]
    query = start + first_query + lax.broadcasted_iota(jnp.int32, (rows, 1), 0)
    low = lowest_key(query, cut)
    key = start + first_key + lax.broadcasted_iota(jnp.int32, (rows, keys), 1)
    mask = (key <= query) & (key >= low)
    mask = jnp.concatenate([mask] * GROUP, 0)
    lanes = head_lanes()
    key_row = first_key + HALO
    for group in range(HEADS // GROUP):
        cols = slice(group * GROUP * HEAD_DIM, (group + 1) * GROUP * HEAD_DIM)
        stacked = stack_heads(q_ref[at_row : at_row + rows, cols], lanes)
        scores = mm_nt(stacked, k_ref[key_row : key_row + keys, cols]) * HEAD_DIM ** (-0.5)
        scores = jnp.where(mask, scores, -1e30)
        exponent = jnp.exp(scores - jnp.max(scores, -1, keepdims=True))
        weights = exponent * (1.0 / jnp.sum(exponent, -1, keepdims=True))
        mixed = mm(weights.astype(bf16), v_ref[key_row : key_row + keys, cols])
        att_ref[at_row : at_row + rows, cols] = unstack_heads(mixed, lanes).astype(bf16)


def front(x, vec_ref, base, w_in, cos_ref, sin_ref, sc_ref, n1_ref, q_ref, k_ref, v_ref, att_ref,
          extra):
    width = x.shape[1]
    normal, _ = normalize(x)
    low = (normal * vec_ref[base : base + 1] + vec_ref[base + 1 : base + 2]).astype(bf16)
    n1_ref[...] = low[HALO:]
    skip = HALO - extra
    queries = mm(low[skip:], w_in[:, :width])
    keys = mm(low, w_in[:, width : 2 * width])
    for at in range(0, width, 128):
        q_ref[:, at : at + 128] = rotate(
            queries[:, at : at + 128], cos_ref[skip:], sin_ref[skip:]
        ).astype(bf16)
        k_ref[:, at : at + 128] = rotate(keys[:, at : at + 128], cos_ref[...], sin_ref[...]).astype(
            bf16
        )
    v_ref[...] = mm(low, w_in[:, 2 * width :]).astype(bf16)
    frames = x.shape[0] - HALO
    if extra:
        attend(q_ref, k_ref, v_ref, att_ref, sc_ref, extra, -extra, -HALO, HALO, 0)
    for first in range(0, frames, QUERIES):
        attend(
            q_ref, k_ref, v_ref, att_ref, sc_ref, QUERIES, first, first - HALO, WINDOW,
            extra + first,
        )


def decoder_front_kernel(sc_ref, *refs):
    pieces, refs = refs[:PIECES], refs[PIECES:]
    (qz_ref, vec_ref, cos_ref, sin_ref, x_ref, restored_ref, n1_ref, q_ref, k_ref, v_ref, att_ref,
     w_vmem, x_scr, sems) = refs
    width = x_ref.shape[1]
    wait_all(fetch(sc_ref, pieces, 0, w_vmem.shape[1], w_vmem, sems))
    latent = qz_ref.shape[1]
    restored = mm_nt(qz_ref[...], w_vmem[:, :latent]).astype(bf16)
    restored_ref[...] = restored[CODE_HALO - 16 :]
    both = mm(restored, w_vmem[:, latent : latent + 4 * width])
    bias = vec_ref[7:8]
    now = both[16:, : 2 * width]
    before = pltpu.roll(both[:, 2 * width :], 1, 0)[16:]
    total = now + before
    x = interleave(total[:, :width] + bias, total[:, width:] + bias, x_scr)
    x_ref[...] = x[HALO:]
    w_in = w_vmem.at[:, latent + 4 * width :]
    front(x, vec_ref, 8, w_in, cos_ref, sin_ref, sc_ref, n1_ref, q_ref, k_ref, v_ref,
          att_ref, 0)


def encoder_front_kernel(sc_ref, *refs):
    (pieces,), refs = split_refs(refs, (PIECES,))
    (halo_ref, x_ref, vec_ref, cos_ref, sin_ref, n1_ref, q_ref, k_ref, v_ref, att_ref,
     w_vmem, sems) = refs
    width = x_ref.shape[1]
    copies = fetch(sc_ref, pieces, 0, 3 * width, w_vmem, sems)
    x = jnp.concatenate([halo_ref[...], x_ref[...]], 0).astype(f32)
    wait_all(copies)
    front(x, vec_ref, 0, w_vmem, cos_ref, sin_ref, sc_ref, n1_ref, q_ref, k_ref, v_ref, att_ref,
          EXTRA)


def gelu_both(hidden):
    share = 0.5 * (1.0 + lax.erf(hidden * 0.7071067811865476))
    density = jnp.exp(-0.5 * hidden * hidden) * 0.3989422804014327
    return hidden * share, share + hidden * density


def l2_rows(w, at, chunk, width):
    rows = width // 4
    return jnp.concatenate(
        [
            w[chunk * rows : (chunk + 1) * rows, at + g * width : at + (g + 1) * width]
            for g in range(4)
        ],
        0,
    )


def fetch_layer(sc_ref, groups, plan, width, w_vmem, sems):
    edges = (0, width, 5 * width, 9 * width)
    return [
        fetch(
            sc_ref, groups[plan[i][0]], plan[i][1], high - low, w_vmem.at[:, low:high], sems,
            PIECES * i,
        )
        for i, (low, high) in enumerate(zip(edges[:-1], edges[1:]))
    ]


def ff_forward(base, extra, copies, w_vmem, att_ref, stream, vec_ref, out_ref, n2_ref, active_ref,
               slope_ref, mid_ref, second_ref, h_scr, act_scr):
    rows, width = stream.shape
    scale_one = vec_ref[base + 2 : base + 3]
    gain_two = vec_ref[base + 3 : base + 4]
    bias_two = vec_ref[base + 4 : base + 5]
    scale_two = vec_ref[base + 5 : base + 6]
    wait_all(copies[0])
    middle = stream + scale_one * mm(att_ref[...], w_vmem[:, :width])
    mid_ref[...] = middle[extra:]
    normal, _ = normalize(middle)
    n2 = (normal * gain_two + bias_two).astype(bf16)
    n2_ref[...] = n2[extra:]
    wait_all(copies[1])
    l1_at, l2_at = width, 5 * width
    second = None
    for chunk in range(4):
        cols = slice(chunk * width, (chunk + 1) * width)
        h_scr[...] = mm(n2, w_vmem[:, l1_at + chunk * width : l1_at + (chunk + 1) * width])
        if extra:
            act, _ = gelu_both(h_scr[:extra, :])
            act_scr[:extra, cols] = act.astype(bf16)

        def body(i, _):
            at_row = pl.multiple_of(i * 16, 16)
            act, slope = gelu_both(h_scr[pl.ds(at_row + extra, 16), :])
            act_scr[pl.ds(at_row + extra, 16), cols] = act.astype(bf16)
            slope_ref[pl.ds(at_row, 16), cols] = slope
            return 0

        lax.fori_loop(0, (rows - extra) // 16, body, 0)
        if chunk == 0:
            wait_all(copies[2])
        part = mm(act_scr[:, cols], l2_rows(w_vmem, l2_at, chunk, width))
        second = part if second is None else second + part
    active_ref[...] = act_scr[extra:, :]
    second_ref[...] = second[extra:]
    out_ref[...] = (middle + scale_two * second).astype(bf16)


def ff_backward(base, extra, w_vmem, att_ref, g, vec_ref, slope_ref, mid_ref, second_ref, gmid_ref,
                dh_ref, dtwo_ref, done_ref, vg_ref, datt_scr):
    width = g.shape[1]
    scale_one = vec_ref[base + 2 : base + 3]
    gain_two = vec_ref[base + 3 : base + 4]
    scale_two = vec_ref[base + 5 : base + 6]
    l1_at, l2_at = width, 5 * width
    vg_ref[3:4, :] = column_sum(g * second_ref[...])
    d_two = (g * scale_two).astype(bf16)
    dtwo_ref[...] = d_two
    e = None
    for chunk in range(4):
        cols = slice(chunk * width, (chunk + 1) * width)
        d_active = mm_nt(d_two, l2_rows(w_vmem, l2_at, chunk, width))
        dh_ref[:, cols] = (d_active * slope_ref[:, cols]).astype(bf16)
        part = mm_nt(
            dh_ref[:, cols], w_vmem[:, l1_at + chunk * width : l1_at + (chunk + 1) * width]
        )
        e = part if e is None else e + part
    normal, scaled = normalize(mid_ref[...])
    vg_ref[1:2, :] = column_sum(e * normal)
    vg_ref[2:3, :] = column_sum(e)
    g_mid = g + norm_backward(e, normal, scaled, gain_two)
    gmid_ref[...] = g_mid
    vg_ref[0:1, :] = column_sum(g_mid * mm(att_ref[extra:, :], w_vmem[:, :width]))
    d_one = (g_mid * scale_one).astype(bf16)
    done_ref[...] = d_one
    datt_scr[...] = mm_nt(d_one, w_vmem[:, :width]).astype(bf16)


def decoder_layer_kernel(plan, sc_ref, *refs):
    (pieces,), refs = split_refs(refs, (PIECES,))
    (att_ref, x_ref, g_ref, vec_ref, q_ref, k_ref, v_ref,
     out_ref, n2_ref, active_ref, gmid_ref, dh_ref, dtwo_ref, done_ref, vg_ref,
     dq_ref, dk_ref, dv_ref, dkv_ref,
     w_vmem, h_scr, act_scr, slope_scr, mid_scr, second_scr, datt_scr, dk_scr, dv_scr, sems) = refs
    width = x_ref.shape[1]
    copies = fetch_layer(sc_ref, (pieces,), plan, width, w_vmem, sems)
    ff_forward(8, 0, copies, w_vmem, att_ref, x_ref[...], vec_ref, out_ref, n2_ref, active_ref,
               slope_scr, mid_scr, second_scr, h_scr, act_scr)
    ff_backward(8, 0, w_vmem, att_ref, g_ref[...].astype(f32), vec_ref, slope_scr, mid_scr,
                second_scr, gmid_ref, dh_ref, dtwo_ref, done_ref, vg_ref, datt_scr)
    attention_backward(0, sc_ref, q_ref, k_ref, v_ref, datt_scr, dq_ref, dk_ref, dv_ref, dkv_ref,
                       dk_scr, dv_scr)


def encoder_forward_kernel(plan, sc_ref, *refs):
    groups, refs = split_refs(refs, (PIECES, PIECES))
    (halo_ref, x_ref, att_ref, vec_ref,
     out_ref, n2_ref, active_ref, slope_ref, mid_ref, second_ref,
     w_vmem, h_scr, act_scr, sems) = refs
    width = x_ref.shape[1]
    copies = fetch_layer(sc_ref, groups, plan, width, w_vmem, sems)
    stream = jnp.concatenate([halo_ref[HALO - EXTRA :, :], x_ref[...]], 0).astype(f32)
    ff_forward(0, EXTRA, copies, w_vmem, att_ref, stream, vec_ref, out_ref, n2_ref, active_ref,
               slope_ref, mid_ref, second_ref, h_scr, act_scr)


def encoder_backward_kernel(plan, sc_ref, *refs):
    groups, refs = split_refs(refs, (PIECES, PIECES))
    (att_ref, g_ref, vec_ref, slope_ref, mid_ref, second_ref, q_ref, k_ref, v_ref,
     gmid_ref, dh_ref, dtwo_ref, done_ref, vg_ref, dq_ref, dk_ref, dv_ref, dkv_ref,
     w_vmem, datt_scr, dk_scr, dv_scr, sems) = refs
    width = g_ref.shape[1]
    for copies in fetch_layer(sc_ref, groups, plan, width, w_vmem, sems):
        wait_all(copies)
    ff_backward(0, EXTRA, w_vmem, att_ref, g_ref[...], vec_ref, slope_ref, mid_ref, second_ref,
                gmid_ref, dh_ref, dtwo_ref, done_ref, vg_ref, datt_scr)
    attention_backward(EXTRA, sc_ref, q_ref, k_ref, v_ref, datt_scr, dq_ref, dk_ref, dv_ref,
                       dkv_ref, dk_scr, dv_scr)


def attention_backward(extra, sc_ref, q_ref, k_ref, v_ref, do_ref,
                       dq_ref, dk_ref, dv_ref, dkv_ref, dk_scr, dv_scr):
    start, cut = sc_ref[0], sc_ref[1]
    frames = do_ref.shape[0]
    lanes = head_lanes()
    scale = HEAD_DIM ** (-0.5)
    dk_scr[...] = jnp.zeros_like(dk_scr)
    dv_scr[...] = jnp.zeros_like(dv_scr)
    wide = GROUP * QUERIES
    for first in range(0, frames, QUERIES):
        lane = lax.broadcasted_iota(jnp.int32, (1, wide), 1) % QUERIES
        query = start + first + lane
        low = lowest_key(query, cut)
        key = start + first - HALO + lax.broadcasted_iota(jnp.int32, (WINDOW, wide), 0)
        mask = (key <= query) & (key >= low)
        for group in range(HEADS // GROUP):
            cols = slice(group * GROUP * HEAD_DIM, (group + 1) * GROUP * HEAD_DIM)
            qs = stack_heads(q_ref[extra + first : extra + first + QUERIES, cols], lanes)
            ds = stack_heads(do_ref[first : first + QUERIES, cols], lanes)
            kw = k_ref[first : first + WINDOW, cols]
            vw = v_ref[first : first + WINDOW, cols]
            scores = jnp.where(mask, mm_nt(kw, qs) * scale, -1e30)
            exponent = jnp.exp(scores - jnp.max(scores, 0, keepdims=True))
            probs = exponent * (1.0 / jnp.sum(exponent, 0, keepdims=True))
            d_probs = mm_nt(vw, ds)
            mean = jnp.sum(probs * d_probs, 0, keepdims=True)
            d_scores = (probs * (d_probs - mean)).astype(bf16)
            dk_scr[first : first + WINDOW, cols] += mm(d_scores, qs)
            dv_scr[first : first + WINDOW, cols] += mm(probs.astype(bf16), ds)
            dq_ref[first : first + QUERIES, cols] = (
                unstack_heads(mm_tn(d_scores, kw), lanes) * scale
            )
    width = dq_ref.shape[1]
    dkv_ref[:, :width] = (dk_scr[:HALO] * scale).astype(bf16)
    dkv_ref[:, width:] = dv_scr[:HALO].astype(bf16)
    dk_ref[...] = dk_scr[HALO:] * scale
    dv_ref[...] = dv_scr[HALO:]


class Packer:
    def __init__(self, core, refs, shares, order):
        self.core, self.refs, self.shares, self.order = core, refs, shares, order

    def put(self, value, at, step=1, phase=0, block0=0):
        if len(self.refs) == 1:
            if step == 1:
                self.refs[0][:, at : at + value.shape[1]] = value.astype(bf16)
            return
        send, keep = self.refs
        cols = slice(at, at + value.shape[1])
        rows = 16
        hi = self.shares // 8
        blocks = value.shape[0] // (rows * step)
        for pair in range(blocks // 2):
            even = value[(2 * pair * step + phase) * rows :][:rows]
            odd = value[((2 * pair + 1) * step + phase) * rows :][:rows]
            block = (block0 + 2 * pair) // 2
            place = {"x": (block % 2, 2), "lo": (block // 2 % 2, 2), "hi": (block // 4, hi)}
            at_row = 0
            for axis in self.order:
                at_row = at_row * place[axis][1] + place[axis][0]
            at_row = at_row * rows
            first = self.core == 0
            keep[at_row : at_row + rows, cols] = jnp.where(first, even, odd).astype(bf16)
            send[at_row : at_row + rows, cols] = jnp.where(first, odd, even).astype(bf16)

    def put_l2(self, value, at, chunk, width):
        if len(self.refs) == 1:
            cols = slice(at + chunk * width, at + (chunk + 1) * width)
            self.refs[0][:, cols] = value.astype(bf16)
            return
        for phase in range(4):
            self.put(value, at + phase * width, 4, phase, chunk * width // 64)


def linear_gradients(pack, n2_ref, active_ref, dh_ref, dtwo_ref):
    width = n2_ref.shape[1]
    for chunk in range(4):
        cols = slice(chunk * width, (chunk + 1) * width)
        pack.put_l2(mm_tn(active_ref[:, cols], dtwo_ref[...]), 0, chunk, width)
        pack.put(mm_tn(n2_ref[...], dh_ref[:, cols]), (4 + chunk) * width)


def decoder_gradients_kernel(shares, sc_ref, n2_ref, active_ref, dh_ref, dtwo_ref, att_ref, done_ref,
                             *refs):
    pack = Packer(sc_ref[2], refs, shares, ORDER_A)
    linear_gradients(pack, n2_ref, active_ref, dh_ref, dtwo_ref)
    pack.put(mm_tn(att_ref[...], done_ref[...]), 8 * n2_ref.shape[1])


def encoder_gradients_kernel(shares, sc_ref, n2_ref, active_ref, dh_ref, dtwo_ref, att_ref, done_ref,
                             win_ref, dred_ref, red_ref, dlat_ref, *refs):
    width = n2_ref.shape[1]
    half = len(refs) // 2
    linear_gradients(
        Packer(sc_ref[2], refs[:half], shares, ORDER_C_ONE), n2_ref, active_ref, dh_ref, dtwo_ref
    )
    pack = Packer(sc_ref[2], refs[half:], shares, ORDER_C_TWO)
    d_reduced = dred_ref[...]
    for tap in range(4):
        pack.put(mm_tn(win_ref[tap], d_reduced), tap * width)
    pack.put(mm_tn(att_ref[EXTRA:, :], done_ref[...]), 4 * width)
    pack.put(mm_tn(red_ref[...], dlat_ref[...]), 5 * width)


def layer_input_gradient(base, dq_ref, dk_ref, dv_ref, dkv_ref, x, gmid_ref,
                         w_in, vec_ref, cos_ref, sin_ref, dmix_ref, vg_ref):
    frames, width = dq_ref.shape
    later = frames - HALO
    cos, sin = cos_ref[HALO:], -sin_ref[HALO:]
    for at in range(0, width, 128):
        cols = slice(at, at + 128)
        dmix_ref[:, cols] = rotate(dq_ref[:, cols], cos, sin).astype(bf16)
        keys = dk_ref[:, cols]
        keys = jnp.concatenate([keys[:later], keys[later:] + dkv_ref[:, cols].astype(f32)], 0)
        dmix_ref[:, width + at : width + at + 128] = rotate(keys, cos, sin).astype(bf16)
        values = dv_ref[:, cols]
        moved = dkv_ref[:, width + at : width + at + 128].astype(f32)
        values = jnp.concatenate([values[:later], values[later:] + moved], 0)
        dmix_ref[:, 2 * width + at : 2 * width + at + 128] = values.astype(bf16)
    d_normed = mm_nt(dmix_ref[...], w_in[...])
    normal, scaled = normalize(x)
    vg_ref[0:1, :] = column_sum(d_normed * normal)
    vg_ref[1:2, :] = column_sum(d_normed)
    return gmid_ref[...] + norm_backward(d_normed, normal, scaled, vec_ref[base : base + 1])


def decoder_back_kernel(at, sc_ref, *refs):
    pieces, refs = refs[:PIECES], refs[PIECES:]
    (dq_ref, dk_ref, dv_ref, dkv_ref, x_ref, gmid_ref, vec_ref, cos_ref, sin_ref,
     dup_ref, dmix_ref, vg_ref, w_vmem, sems) = refs
    wait_all(fetch(sc_ref, pieces, at, w_vmem.shape[1], w_vmem, sems))
    grad = layer_input_gradient(
        8, dq_ref, dk_ref, dv_ref, dkv_ref, x_ref[...], gmid_ref, w_vmem, vec_ref,
        cos_ref, sin_ref, dmix_ref, vg_ref,
    )
    vg_ref[2:3, :] = column_sum(grad)
    dup_ref[...] = grad.astype(bf16)


def encoder_back_kernel(shares, sc_ref, *refs):
    (pieces,), refs = split_refs(refs, (PIECES,))
    (dq_ref, dk_ref, dv_ref, dkv_ref, x_ref, gmid_ref, vec_ref, cos_ref, sin_ref, n1_ref,
     vgs_ref, grad_ref, *rest) = refs
    refs, (w_vmem, dmix_scr, vg_scr, all_scr, sems) = rest[:-5], rest[-5:]
    width = x_ref.shape[1]
    wait_all(fetch(sc_ref, pieces, 0, w_vmem.shape[1], w_vmem, sems))
    grad = layer_input_gradient(
        0, dq_ref, dk_ref, dv_ref, dkv_ref, x_ref[...].astype(f32), gmid_ref, w_vmem,
        vec_ref, cos_ref, sin_ref, dmix_scr, vg_scr,
    )
    grad_ref[...] = grad.astype(bf16)
    pack = Packer(sc_ref[2], refs, shares, ORDER_D)
    for part in range(3):
        cols = slice(part * width, (part + 1) * width)
        pack.put(mm_tn(n1_ref[...], dmix_scr[:, cols]), part * width)
    all_scr[...] = jnp.zeros_like(all_scr)
    all_scr[0:2, :] = vg_scr[0:2, :]
    all_scr[2:6, :] = vgs_ref[0:4, :]
    all_scr[6:7, :] = vgs_ref[16:17, :]
    all_scr[7:8, :] = vgs_ref[26:27, :]
    all_scr[8:10, :] = vgs_ref[24:26, :]
    all_scr[10:14, :] = vgs_ref[8:12, :]
    pack.put(all_scr[...].T, 3 * width)


def middle_kernel(shares, sc_ref, *refs):
    (pieces, more), refs = split_refs(refs, (PIECES, PIECES))
    (dup_ref, next_ref, dmix_ref, n1_ref, restored_ref, qz_ref,
     denc_ref, dred_ref, dlat_ref, vg_ref, *rest) = refs
    refs, (up_vmem, down_vmem, frame_scr, sems) = rest[:-4], rest[-4:]
    frames, width = dup_ref.shape
    latent = qz_ref.shape[1]
    codec = frames // 2
    copies = [
        fetch(sc_ref, pieces, 0, latent + 4 * width, up_vmem, sems),
        fetch(sc_ref, more, 4 * width, 4 * width + latent, down_vmem, sems, PIECES),
    ]
    pairs = codec + 16
    even, odd = split_rows(
        jnp.concatenate([dup_ref[...], next_ref[...]], 0).astype(f32), frame_scr
    )
    both = jnp.concatenate([even, odd], 1).astype(bf16)
    wait_all(copies[0])
    up = up_vmem[:, latent : latent + 4 * width]
    here = mm_nt(both, up[:, : 2 * width])
    later = mm_nt(both, up[:, 2 * width :])
    d_restored = (here + pltpu.roll(later, pairs - 1, 0)).astype(bf16)
    d_latent = mm(d_restored, up_vmem[:, :latent]).astype(bf16)
    wait_all(copies[1])
    d_reduced = mm_nt(d_latent, down_vmem[:, 4 * width :]).astype(bf16)
    dlat_ref[...] = d_latent[:codec]
    dred_ref[...] = d_reduced[:codec]
    vg_ref[0:1, :] = column_sum(d_reduced[:codec].astype(f32))
    taps = [mm_nt(d_reduced, down_vmem[:, tap * width : (tap + 1) * width]) for tap in range(4)]
    denc_ref[...] = interleave(
        taps[2] + pltpu.roll(taps[0], pairs - 1, 0),
        taps[3] + pltpu.roll(taps[1], pairs - 1, 0),
        frame_scr,
    )[:frames]

    pack = Packer(sc_ref[2], refs, shares, ORDER_B)
    for part in range(3):
        cols = slice(part * width, (part + 1) * width)
        pack.put(mm_tn(n1_ref[...], dmix_ref[:, cols]), part * width)
    restored = restored_ref[...]
    own_pairs = both[:codec]
    before = pltpu.roll(restored.astype(f32), 1, 0)[16:].astype(bf16)
    pack.put(mm_tn(restored[16:], own_pairs[:, :width]), 3 * width)
    pack.put(mm_tn(restored[16:], own_pairs[:, width:]), 4 * width)
    pack.put(mm_tn(before, own_pairs[:, :width]), 5 * width)
    pack.put(mm_tn(before, own_pairs[:, width:]), 6 * width)
    pack.put(mm_tn(d_restored[:codec], qz_ref[CODE_HALO:, :]), 7 * width)


def latent_kernel(sc_ref, *refs):
    (pieces,), refs = split_refs(refs, (PIECES,))
    (enc_ref, rows_ref, vec_ref, res_ref, win_ref, red_ref, w_vmem, frame_scr, sems) = refs
    total, width = enc_ref.shape
    copies = fetch(sc_ref, pieces, 4 * width, w_vmem.shape[1], w_vmem, sems)
    inside = (sc_ref[0] > 0).astype(f32)
    rim = enc_ref[:EXTRA].astype(f32) * inside
    skip = EXTRA // 2
    even, odd = split_rows(jnp.concatenate([rim, enc_ref[EXTRA:].astype(f32)], 0), frame_scr)
    win_ref[0] = pltpu.roll(even, 1, 0)[skip:].astype(bf16)
    win_ref[1] = pltpu.roll(odd, 1, 0)[skip:].astype(bf16)
    win_ref[2] = even[skip:].astype(bf16)
    win_ref[3] = odd[skip:].astype(bf16)
    wait_all(copies)
    reduced = vec_ref[6:7]
    for tap in range(4):
        reduced = reduced + mm(win_ref[tap], w_vmem[:, tap * width : (tap + 1) * width])
    reduced = reduced.astype(bf16)
    red_ref[...] = reduced
    remaining = mm(reduced, w_vmem[:, 4 * width :])
    for level in range(rows_ref.shape[0]):
        res_ref[level] = remaining.astype(bf16)
        remaining = remaining - rows_ref[level].astype(f32)


def lookup_kernel(sc_ref, codes_ref, book_ref, qsend_ref, qkeep_ref, rsend_ref, rkeep_ref, q_scr):
    levels, share, latent = book_ref.shape
    total = codes_ref.shape[0]
    codec = total // 4
    base = sc_ref[3]
    core = sc_ref[2]
    entry = lax.broadcasted_iota(jnp.int32, (1, share), 1)
    for level in range(levels):
        picks = (codes_ref[:, level : level + 1] - base == entry).astype(f32).astype(bf16)
        found = mm(picks, book_ref[level])
        q_scr[CODE_HALO:] = found if level == 0 else q_scr[CODE_HALO:] + found
        for x in range(2):
            even = found[(2 * x) * codec :][:codec]
            odd = found[(2 * x + 1) * codec :][:codec]
            rkeep_ref[x, level] = jnp.where(core == 0, even, odd).astype(bf16)
            rsend_ref[x, level] = jnp.where(core == 0, odd, even).astype(bf16)
    q_scr[:CODE_HALO] = jnp.zeros((CODE_HALO, latent), f32)
    for x in range(2):
        even = q_scr[(2 * x) * codec : (2 * x + 1) * codec + CODE_HALO]
        odd = q_scr[(2 * x + 1) * codec : (2 * x + 2) * codec + CODE_HALO]
        qkeep_ref[x] = jnp.where(core == 0, even, odd)
        qsend_ref[x] = jnp.where(core == 0, odd, even)


def collect_kernel(share, seq_count, sc_ref, own_ref, x_ref, core_ref, far_ref, codes_ref,
                   marked_ref, send_ref, keep_ref, row_scr, cnt_scr):
    levels, codec, latent = own_ref.shape
    total = codes_ref.shape[1]
    lo = sc_ref[4]
    high = send_ref.shape[0]
    frame = lax.broadcasted_iota(jnp.int32, (1, total), 1) + sc_ref[6]
    row = lax.broadcasted_iota(jnp.int32, (2 * high * share, 1), 0)
    entry = (row // share * seq_count + sc_ref[5]) * share + row % share
    ones = jnp.ones((16, total), bf16)
    for level in range(levels):
        marked = marked_ref[:, level : level + 1]
        used = (entry == codes_ref[level : level + 1, :]).astype(f32)
        placed = (marked // 2 == frame).astype(f32)
        select = jnp.where(marked % 2 == 1, placed, used).astype(bf16)
        for place, ref in enumerate((own_ref, x_ref, core_ref, far_ref)):
            at_row = pl.multiple_of(sc_ref[14 + place], 32)
            row_scr[pl.ds(at_row, codec), :] = ref[level]
        sums = mm(select, row_scr[...])
        cnt_scr[level : level + 1, :] = mm_nt(ones, used.astype(bf16))[0:1]
        at = slice(level * share, (level + 1) * share)
        for h in range(high):
            even = sums[(2 * h) * share :][:share]
            odd = sums[(2 * h + 1) * share :][:share]
            keep_ref[h, at, :] = jnp.where(lo == 0, even, odd).astype(bf16)
            send_ref[h, at, :] = jnp.where(lo == 0, odd, even).astype(bf16)
    counts = cnt_scr[...]
    upper = jnp.floor(counts * (1.0 / 128.0))
    digits = jnp.concatenate([upper, counts - 128.0 * upper], 0)
    tail = slice(levels * share, levels * share + 2 * levels)
    for h in range(high):
        even = digits[:, (2 * h) * share : (2 * h + 1) * share]
        odd = digits[:, (2 * h + 1) * share : (2 * h + 2) * share]
        keep_ref[h, tail, :] = jnp.zeros((2 * levels, latent), bf16)
        send_ref[h, tail, :] = jnp.zeros((2 * levels, latent), bf16)
        keep_ref[h, tail, :share] = jnp.where(lo == 0, even, odd).astype(bf16)
        send_ref[h, tail, :share] = jnp.where(lo == 0, odd, even).astype(bf16)


def call(kernel, outs, spaces, scratch, args, micros):
    where = {"s": pltpu.SMEM, "v": pltpu.VMEM, "h": pltpu.HBM}
    title = getattr(kernel, "func", kernel).__name__
    return pl.pallas_call(
        kernel,
        name=title,
        out_shape=outs,
        in_specs=[pl.BlockSpec(memory_space=where[space]) for space in spaces],
        out_specs=[pl.BlockSpec(memory_space=pltpu.VMEM) for _ in outs],
        scratch_shapes=scratch,
        compiler_params=pltpu.CompilerParams(vmem_limit_bytes=VMEM_LIMIT),
        cost_estimate=pl.CostEstimate(
            flops=int(micros * 1e6), bytes_accessed=1, transcendentals=0
        ),
    )(*args)


def shape(dims, dtype=f32):
    return jax.ShapeDtypeStruct(dims, dtype)


def pick(block, at):
    zero = jnp.zeros((), jnp.uint32)
    start = (at,) + (zero,) * (block.ndim - 1)
    return lax.dynamic_slice(block, start, (1,) + block.shape[1:])[0]


def halve(block, axis, index, after=None):
    sent = pick(block, index["other " + axis])
    kept = pick(block, index[axis])
    got = lax.ppermute(sent, axis, [(0, 1), (1, 0)])
    if after is not None:
        got, _ = tie(got, after)
    return (kept.astype(f32) + got.astype(f32)).astype(block.dtype)


def sum_by_permutes(block, index, after=None):
    count = block.shape[0]
    if count != 4:
        return sum_over_hi(block)
    total = pick(block, index["hi"]).astype(f32)
    for turn in range(1, count):
        sent = pick(block, index["hi ^ %d" % turn])
        got = lax.ppermute(sent, "hi", [(i, i ^ turn) for i in range(count)])
        if after is not None:
            got, _ = tie(got, after)
        total = total + got.astype(f32)
    return total


def swap_add(send, keep, axis, after=None):
    got = lax.ppermute(send, axis, [(0, 1), (1, 0)])
    if after is not None:
        got, _ = tie(got, after)
    return (keep.astype(f32) + got.astype(f32)).astype(keep.dtype)


def sum_over_hi(block):
    parts = lax.all_to_all(block, "hi", 0, 0, tiled=True)
    return jnp.sum(parts.astype(f32), 0)


def shifted(block, distance):
    devices = range(lax.axis_size(SEQ))
    route = [(i - distance, i) for i in devices if i - distance in devices]
    return lax.ppermute(block, SEQ, route)


def packed_outs(width_total, width, shares):
    if width // shares % 16 == 0:
        return [shape((width // 2, width_total), bf16)] * 2
    return [shape((width, width_total), bf16)]


def swap(block, axis):
    return lax.ppermute(block, axis, [(0, 1), (1, 0)])


def tie(*values):
    return lax.optimization_barrier(values)


def half_of(share, index):
    rows = share.shape[0] // 2
    zero = jnp.zeros((), jnp.uint32)
    return lax.dynamic_slice(share, (index["lo"] * rows, zero), (rows, share.shape[1]))


def both_halves(near, far, index):
    first = index["lo"] == 0
    return jnp.concatenate([jnp.where(first, near, far), jnp.where(first, far, near)], 0)


def unfolded_rows(block, shares, l2_at):
    width = block.shape[0]
    full = [block[:, l2_at + i * width : l2_at + (i + 1) * width] for i in range(4)]
    full = jnp.concatenate(full, 0).reshape(shares, 4, width // shares, width)
    full = full.transpose(0, 2, 1, 3).reshape(width, 4 * width)
    return jnp.concatenate([block[:, :l2_at], full, block[:, l2_at + 4 * width :]], 1)


def first_sum(parts, shares, order, index, l2_at=None):
    if len(parts) == 2:
        return swap_add(*parts, "core")
    (block,) = parts
    if l2_at is not None:
        block = unfolded_rows(block, shares, l2_at)
    width, total = block.shape
    block = block.reshape(shares // 8, 2, 2, 2, width // shares, total)
    block = halve(block.transpose(3, 0, 1, 2, 4, 5), "core", index)
    places = [("hi", "lo", "x").index(axis) for axis in order]
    return block.transpose(*places, 3, 4).reshape(width // 2, total)


def next_sum(block, axis, index, after=None):
    rows, total = block.shape
    return halve(block.reshape(2, rows // 2, total), axis, index, after)


def last_sum(block, high):
    return sum_over_hi(block.reshape(high, -1, block.shape[1]))


def local(
    activations,
    encoder_attention_norm_gain,
    encoder_attention_norm_bias,
    encoder_query_key_value_weight,
    encoder_attention_output_weight,
    encoder_attention_layer_scale,
    encoder_forward_norm_gain,
    encoder_forward_norm_bias,
    encoder_forward_input_weight,
    encoder_forward_output_weight,
    encoder_forward_layer_scale,
    strided_convolution_weight,
    strided_convolution_bias,
    quantizer_input_weight,
    codebook,
    quantizer_output_weight,
    transposed_convolution_weight,
    transposed_convolution_bias,
    decoder_attention_norm_gain,
    decoder_attention_norm_bias,
    decoder_query_key_value_weight,
    decoder_attention_output_weight,
    decoder_attention_layer_scale,
    decoder_forward_norm_gain,
    decoder_forward_norm_bias,
    decoder_forward_input_weight,
    decoder_forward_output_weight,
    decoder_forward_layer_scale,
    cotangent,
    frame_segment_index,
    frame_code_index,
    replace_code_mask,
    replacing_batch_position,
    code_usage_average,
    code_latent_sum_average,
):
    batch_rows, frames, width = activations.shape
    assert batch_rows == 1
    seq_index = lax.axis_index(SEQ)
    seq_count = lax.axis_size(SEQ)
    dp_index = lax.axis_index(DP)
    dp_count = lax.axis_size(DP)
    shares = dp_count * seq_count
    codec = frames // 2
    levels = frame_code_index.shape[2]
    latent = codebook.shape[2]
    book_share = codebook.shape[1]
    core_index = lax.axis_index("core")

    x_index, lo_index = lax.axis_index("x"), lax.axis_index("lo")
    rows_share = width // seq_count
    high = shares // 8
    total_frames = HALO + frames
    code_total = replace_code_mask.shape[1]
    code_share = code_usage_average.shape[1]
    row_frames = codec * seq_count

    vectors = jnp.stack(
        [
            encoder_attention_norm_gain,
            encoder_attention_norm_bias,
            encoder_attention_layer_scale,
            encoder_forward_norm_gain,
            encoder_forward_norm_bias,
            encoder_forward_layer_scale,
            strided_convolution_bias,
            transposed_convolution_bias,
            decoder_attention_norm_gain,
            decoder_attention_norm_bias,
            decoder_attention_layer_scale,
            decoder_forward_norm_gain,
            decoder_forward_norm_bias,
            decoder_forward_layer_scale,
        ]
    )
    vectors = jnp.pad(vectors, ((0, 2), (0, 0)))
    small = jnp.concatenate(
        [frame_code_index.reshape(-1).astype(f32), vectors.reshape(-1).astype(f32)]
    )
    index = {}
    unsigned = jnp.uint32
    for axis in ("x", "lo", "core"):
        index[axis] = lax.axis_index(axis).astype(unsigned)
        index["other " + axis] = (1 - lax.axis_index(axis)).astype(unsigned)
    index["hi"] = lax.axis_index("hi").astype(unsigned)
    index["seq"] = lax.axis_index(SEQ).astype(unsigned)
    index["owner"] = (lax.axis_index(DP + SEQ) * code_share).astype(unsigned)
    for turn in range(1, 4):
        index["hi ^ %d" % turn] = lax.axis_index("hi").astype(unsigned) ^ unsigned(turn)
    def flat_taps(taps):
        return taps.transpose(1, 0, 2).reshape(taps.shape[1], -1)

    def fold_l2(share):
        return share.reshape(4, -1, width).transpose(1, 0, 2).reshape(-1, 4 * width)

    dec_one = jnp.concatenate(
        [
            quantizer_output_weight.T,
            flat_taps(transposed_convolution_weight),
            decoder_query_key_value_weight,
        ],
        1,
    )
    half_one = half_of(dec_one, index)
    small, half_one = tie(small, half_one)
    small = lax.all_gather(small, SEQ, axis=0, tiled=False)
    names = sorted(index)
    *index_values, small = tie(*[index[name] for name in names], small)
    index = dict(zip(names, index_values))
    code_count = codec * levels
    row_codes = small[:, :code_count].astype(jnp.int32).reshape(seq_count, codec, levels)
    vectors = small[:, code_count:].reshape(seq_count, 16, -1).transpose(1, 0, 2).reshape(16, width)
    order = [2 * x_index + core_index, 2 * (1 - x_index) + core_index]
    order += [2 * x_index + 1 - core_index, 2 * (1 - x_index) + 1 - core_index]
    cut = jnp.sum((frame_segment_index[0] == 0).astype(jnp.int32))
    scalars = jnp.stack(
        [
            seq_index * frames,
            cut,
            core_index,
            seq_index * book_share,
            lo_index,
            seq_index,
            dp_index * row_frames,
            seq_index,
        ]
        + [
            *[place * rows_share for place in order],
            seq_index,
            seq_index,
        ]
        + [place * codec for place in order]
    ).astype(jnp.int32)

    half_one, _ = tie(half_one, small)
    near_one = swap(half_one, "x")
    core_one = swap(dec_one, "core")
    activation_halo = shifted(activations[0, frames - HALO :], 1)

    positions = seq_index * frames - HALO + jnp.arange(total_frames, dtype=jnp.int32)
    half_dim = HEAD_DIM // 2
    frequency = jnp.power(10000.0, -jnp.arange(half_dim, dtype=f32) / half_dim)

    def angle_tables(positions):
        angles = positions.astype(f32)[:, None] * frequency[None, :]
        cos, sin = jnp.cos(angles), jnp.sin(angles)
        return jnp.concatenate([cos] * 4, 1), jnp.concatenate([-sin, sin, -sin, sin], 1)

    row_codes, activation_halo, core_one = tie(row_codes, activation_halo, core_one)

    window = codec + CODE_HALO
    qsend, qkeep, rsend, rkeep = call(
        lookup_kernel,
        [shape((2, window, latent))] * 2 + [shape((2, levels, codec, latent), bf16)] * 2,
        "svv",
        [pltpu.VMEM((CODE_HALO + codec * seq_count, latent), f32)],
        (scalars, row_codes.reshape(-1, levels), codebook),
        4,
    )
    q_sum = swap_add(qsend, qkeep, "core")
    q_sent = pick(q_sum, index["other x"])
    q_got = swap(q_sent, "x")
    (near_one, positions, dec_l2, enc_in, enc_l2, down_share, replace_code_mask,
     replacing_batch_position, row_codes, _) = tie(
        near_one, positions, decoder_forward_output_weight, encoder_query_key_value_weight,
        encoder_forward_output_weight, strided_convolution_weight, replace_code_mask,
        replacing_batch_position, row_codes, q_sent,
    )
    dec_two = jnp.concatenate(
        [decoder_attention_output_weight, decoder_forward_input_weight, fold_l2(dec_l2)], 1
    )
    enc_one = jnp.concatenate(
        [
            enc_in,
            encoder_attention_output_weight,
            flat_taps(down_share),
            quantizer_input_weight,
        ],
        1,
    )
    marked = (replacing_batch_position * 2 + replace_code_mask).T
    marked = marked.reshape(dp_count, seq_count, code_share, levels).transpose(1, 0, 2, 3)
    marked = pick(marked, index["seq"]).reshape(dp_count * code_share, levels)
    code_columns = row_codes.reshape(row_frames, levels).T
    owner_flag = lax.dynamic_slice(
        replace_code_mask, (jnp.zeros((), unsigned), index["owner"]), (levels, code_share)
    ) == 1
    far_one = swap(near_one, "lo")
    near_one = both_halves(near_one, far_one, index)
    dec_one = [dec_one, near_one, core_one, swap(near_one, "core")]
    half_two = half_of(dec_two, index)
    cos_table, sin_table = angle_tables(positions)
    near_two = swap(half_two, "x")
    quantized = (pick(q_sum, index["x"]) + q_got).astype(bf16)
    half_three = half_of(enc_one, index)
    (quantized, near_two, half_three, activation_halo, cos_table, sin_table, marked,
     code_columns, owner_flag) = tie(
        quantized, near_two, half_three, activation_halo, cos_table, sin_table, marked,
        code_columns, owner_flag,
    )
    core_two = swap(dec_two, "core")
    far_two = swap(near_two, "lo")
    near_three = swap(half_three, "x")

    d_x, restored, d_n1, d_q, d_k, d_v, d_att = call(
        decoder_front_kernel,
        [
            shape((frames, width)),
            shape((codec + 16, width), bf16),
            shape((frames, width), bf16),
            shape((frames, width), bf16),
            shape((total_frames, width), bf16),
            shape((total_frames, width), bf16),
            shape((frames, width), bf16),
        ],
        "s" + "h" * PIECES + "vvvv",
        [
            pltpu.VMEM((width, latent + 7 * width), bf16),
            pltpu.VMEM((width // 128, total_frames, 128), f32),
            pltpu.SemaphoreType.DMA((PIECES,)),
        ],
        (scalars, *dec_one, quantized, vectors, cos_table, sin_table),
        8,
    )
    d_att, far_two, near_three, enc_l2, rsend = tie(d_att, far_two, near_three, enc_l2, rsend)
    enc_two = jnp.concatenate([encoder_forward_input_weight, fold_l2(enc_l2)], 1)
    half_four = half_of(enc_two, index)
    code_rows = swap_add(rsend, rkeep, "core")
    near_two = both_halves(near_two, far_two, index)
    dec_two = [dec_two, near_two, core_two, swap(near_two, "core")]
    far_three = swap(near_three, "lo")
    near_four = swap(half_four, "x")
    layer_scratch = [
        pltpu.VMEM((frames, width), bf16),
        pltpu.VMEM((total_frames, width), f32),
        pltpu.VMEM((total_frames, width), f32),
        pltpu.SemaphoreType.DMA((3 * PIECES,)),
    ]
    forward_outs = [shape((frames, width), bf16), shape((frames, 4 * width), bf16)]
    kept_outs = [shape((frames, 4 * width)), shape((frames, width)), shape((frames, width))]
    backward_outs = [
        shape((frames, width)),
        shape((frames, 4 * width), bf16),
        shape((frames, width), bf16),
        shape((frames, width), bf16),
        shape((8, width)),
        shape((frames, width)),
        shape((frames, width)),
        shape((frames, width)),
        shape((HALO, 2 * width), bf16),
    ]
    weights_scratch = pltpu.VMEM((width, 9 * width), bf16)
    (output, d_n2, d_active, d_gmid, d_dh, d_dtwo, d_done, d_vg_two, d_dq, d_dk, d_dv, d_dkv) = call(
        partial(decoder_layer_kernel, ((0, 0), (0, width), (0, 5 * width))),
        [shape((frames, width), bf16)] + forward_outs + backward_outs,
        "s" + "h" * PIECES + "vvvvvvv",
        [
            weights_scratch,
            pltpu.VMEM((frames, width), f32),
            pltpu.VMEM((frames, 4 * width), bf16),
            pltpu.VMEM((frames, 4 * width), f32),
            pltpu.VMEM((frames, width), f32),
            pltpu.VMEM((frames, width), f32),
        ]
        + layer_scratch,
        (scalars, *dec_two, d_att, d_x, cotangent[0], vectors, d_q, d_k, d_v),
        14,
    )
    d_n2, far_three, near_four, code_rows = tie(d_n2, far_three, near_four, code_rows)
    near_three = both_halves(near_three, far_three, index)
    enc_one = [enc_one, near_three, swap(enc_one, "core"), swap(near_three, "core")]
    far_four = swap(near_four, "lo")
    d_dkv = shifted(d_dkv, -1)
    group_a = call(
        partial(decoder_gradients_kernel, shares),
        packed_outs(9 * width, width, shares),
        "svvvvvv",
        [],
        (scalars, d_n2, d_active, d_dh, d_dtwo, d_att, d_done),
        5,
    )
    d_dq, *group_a = tie(d_dq, *group_a)
    code_rows, d_dkv = tie(code_rows, d_dkv)
    code_rows = halve(code_rows, "x", index)
    a_sum = first_sum(group_a, shares, ORDER_A, index, 0)
    d_up, d_mixed, d_vg_one = call(
        partial(decoder_back_kernel, latent + 4 * width),
        [shape((frames, width), bf16), shape((frames, 3 * width), bf16), shape((8, width))],
        "s" + "h" * PIECES + "v" * 9,
        [pltpu.VMEM((width, 3 * width), bf16), pltpu.SemaphoreType.DMA((PIECES,))],
        (
            scalars, *dec_one, d_dq, d_dk, d_dv, d_dkv, d_x, d_gmid, vectors, cos_table,
            sin_table,
        ),
        4,
    )
    d_up_next = shifted(d_up[:32], -1)


    a_sum, d_up, e_input, far_four, code_rows = tie(
        a_sum, d_up, activations[0], far_four, code_rows
    )
    near_four = both_halves(near_four, far_four, index)
    enc_two = [enc_two, near_four, swap(enc_two, "core"), swap(near_four, "core")]
    a_sum = next_sum(a_sum, ORDER_A[0], index)
    e_n1, e_q, e_k, e_v, e_att = call(
        encoder_front_kernel,
        [
            shape((frames, width), bf16),
            shape((frames + EXTRA, width), bf16),
            shape((total_frames, width), bf16),
            shape((total_frames, width), bf16),
            shape((frames + EXTRA, width), bf16),
        ],
        "s" + "h" * PIECES + "vvvvv",
        [pltpu.VMEM((width, 3 * width), bf16), pltpu.SemaphoreType.DMA((PIECES,))],
        (scalars, *enc_one, activation_halo, e_input, vectors, cos_table, sin_table),
        7,
    )

    d_mixed, e_n1 = tie(d_mixed, e_n1)
    middle_outs = call(
        partial(middle_kernel, shares),
        [
            shape((frames, width)),
            shape((codec, width), bf16),
            shape((codec, latent), bf16),
            shape((8, width)),
        ]
        + packed_outs(7 * width + latent, width, shares),
        "s" + "h" * (2 * PIECES) + "" + "v" * 6,
        [
            pltpu.VMEM((width, latent + 4 * width), bf16),
            pltpu.VMEM((width, latent + 4 * width), bf16),
            pltpu.VMEM((width // 128, frames + 32, 128), f32),
            pltpu.SemaphoreType.DMA((2 * PIECES,)),
        ],
        (scalars, *dec_one, *enc_one, d_up, d_up_next, d_mixed, d_n1, restored, quantized),
        7,
    )
    d_encoded, d_reduced, d_latent, m_vg = middle_outs[:4]
    b_sum = first_sum(middle_outs[4:], shares, ORDER_B, index)

    e_att, d_encoded = tie(e_att, d_encoded)
    enc_plan = ((0, 3 * width), (1, 0), (1, 4 * width))
    rows = frames + EXTRA
    encoded, e_n2, e_active, e_slope, e_mid, e_second = call(
        partial(encoder_forward_kernel, enc_plan),
        [shape((rows, width), bf16)] + forward_outs + kept_outs,
        "s" + "h" * (2 * PIECES) + "vvvv",
        [
            weights_scratch,
            pltpu.VMEM((rows, width), f32),
            pltpu.VMEM((rows, 4 * width), bf16),
            pltpu.SemaphoreType.DMA((3 * PIECES,)),
        ],
        (scalars, *enc_one, *enc_two, activation_halo, e_input, e_att, vectors),
        6,
    )
    encoded, b_sum, a_sum = tie(encoded, b_sum, a_sum)
    b_sum = next_sum(b_sum, ORDER_B[0], index)
    residuals, windows, reduced = call(
        latent_kernel,
        [
            shape((levels, codec, latent), bf16),
            shape((4, codec, width), bf16),
            shape((codec, width), bf16),
        ],
        "s" + "h" * PIECES + "vvv",
        [
            pltpu.VMEM((width, 4 * width + latent), bf16),
            pltpu.VMEM((width // 128, frames + EXTRA, 128), f32),
            pltpu.SemaphoreType.DMA((PIECES,)),
        ],
        (scalars, *enc_one, encoded, code_rows, vectors),
        3,
    )
    near_res = swap(residuals, "x")
    core_res = swap(residuals, "core")

    d_encoded, _ = tie(d_encoded, residuals)
    a_sum = next_sum(a_sum, ORDER_A[1], index)
    (e_gmid, e_dh, e_dtwo, e_done, e_vg_two, e_dq, e_dk, e_dv, e_dkv) = call(
        partial(encoder_backward_kernel, enc_plan),
        backward_outs,
        "s" + "h" * (2 * PIECES) + "v" * 9,
        [weights_scratch] + layer_scratch,
        (
            scalars, *enc_one, *enc_two, e_att, d_encoded, vectors, e_slope, e_mid, e_second,
            e_q, e_k, e_v,
        ),
        11,
    )
    e_dkv = shifted(e_dkv, -1)
    near_res, core_res, _ = tie(near_res, core_res, e_gmid)
    res_pieces = [residuals, near_res, core_res, swap(near_res, "core")]

    code_columns, b_sum = tie(code_columns, b_sum)
    if code_share % 16 == 0:
        tail_rows = levels * code_share
        csend, ckeep = call(
            partial(collect_kernel, code_share, seq_count),
            [shape((dp_count // 2, tail_rows + 2 * levels, latent), bf16)] * 2,
            "svvvvvv",
            [
                pltpu.VMEM((row_frames, latent), bf16),
                pltpu.VMEM((levels, dp_count * code_share), f32),
            ],
            (scalars, *res_pieces, code_columns, marked),
            5,
        )
        e_n2, csend, e_gmid, e_dkv = tie(e_n2, csend, e_gmid, e_dkv)
    c_outs = packed_outs(8 * width, width, shares)
    group_c = call(
        partial(encoder_gradients_kernel, shares),
        c_outs + packed_outs(5 * width + latent, width, shares),
        "s" + "v" * 10,
        [],
        (
            scalars, e_n2, e_active, e_dh, e_dtwo, e_att, e_done, windows, d_reduced, reduced,
            d_latent,
        ),
        5,
    )
    e_dq, *group_c = tie(e_dq, *group_c)
    c_one = first_sum(group_c[: len(c_outs)], shares, ORDER_C_ONE, index, 0)
    c_two = first_sum(group_c[len(c_outs) :], shares, ORDER_C_TWO, index)
    e_dq, c_one, c_two, a_sum, b_sum = tie(e_dq, c_one, c_two, a_sum, b_sum)
    vector_grads = jnp.concatenate([e_vg_two, d_vg_two, m_vg, d_vg_one], 0)
    grad_outs = call(
        partial(encoder_back_kernel, shares),
        [shape((frames, width), bf16)] + packed_outs(3 * width + 128, width, shares),
        "s" + "h" * PIECES + "v" * 11,
        [
            pltpu.VMEM((width, 3 * width), bf16),
            pltpu.VMEM((frames, 3 * width), bf16),
            pltpu.VMEM((8, width), f32),
            pltpu.VMEM((128, width), f32),
            pltpu.SemaphoreType.DMA((PIECES,)),
        ],
        (
            scalars, *enc_one, e_dq, e_dk, e_dv, e_dkv, e_input, e_gmid, vectors,
            cos_table, sin_table, e_n1, vector_grads,
        ),
        5,
    )
    activations_grad = grad_outs[0]

    def z_sum(block):
        return sum_by_permutes(block.reshape(high, -1, block.shape[1]), index, activations_grad)

    d_sum = first_sum(grad_outs[1:], shares, ORDER_D, index)
    b_sum = next_sum(b_sum, ORDER_B[1], index, d_sum)
    if code_share % 16 == 0:
        combined = swap_add(csend, ckeep, "lo", b_sum)
        c_one = next_sum(c_one, ORDER_C_ONE[0], index, combined)
        together = last_sum(jnp.concatenate([a_sum, b_sum], 1), high)
        combined, together = tie(combined, together)
        combined = sum_over_hi(combined)
        summed = combined[:tail_rows].reshape(levels, code_share, latent)
        digits = combined[tail_rows:, :code_share]
        counted = 128.0 * digits[:levels] + digits[levels:]
    else:
        entry = (
            jnp.arange(dp_count, dtype=jnp.int32)[:, None] * seq_count + seq_index
        ) * code_share + jnp.arange(code_share, dtype=jnp.int32)
        relative = [place * codec + jnp.arange(codec, dtype=jnp.int32) for place in order]
        relative = jnp.concatenate(relative)
        flat_res = jnp.concatenate(res_pieces, 1)
        used = entry.reshape(1, -1, 1) == code_columns[:, None, relative]
        placed = (marked.T // 2)[:, :, None] == dp_index * row_frames + relative
        counts = jnp.sum(used.astype(f32), 2).reshape(levels, dp_count, code_share)
        selects = jnp.where((marked.T % 2)[:, :, None] == 1, placed, used).astype(bf16)
        sums = jnp.einsum("lct,ltd->lcd", selects, flat_res, preferred_element_type=f32)
        sums = sums.astype(bf16).reshape(levels, dp_count, code_share, latent)
        together = last_sum(jnp.concatenate([a_sum, b_sum], 1), high)
        c_one = next_sum(c_one, ORDER_C_ONE[0], index)
        summed = lax.psum_scatter(sums, DP, scatter_dimension=1, tiled=False).astype(f32)
        counted = lax.psum_scatter(counts, DP, scatter_dimension=1, tiled=False)
    c_two = next_sum(c_two, ORDER_C_TWO[0], index, c_one)
    d_sum = next_sum(d_sum, ORDER_D[0], index, c_two)
    c_two = next_sum(c_two, ORDER_C_TWO[1], index, d_sum)
    d_sum = next_sum(d_sum, ORDER_D[1], index, c_two)
    c_one = next_sum(c_one, ORDER_C_ONE[1], index, d_sum)
    grads_a, grads_b = together[:, : a_sum.shape[1]], together[:, a_sum.shape[1] :]
    edge, far_edge = c_one.shape[1], c_one.shape[1] + c_two.shape[1]
    together = last_sum(jnp.concatenate([c_one, c_two, d_sum], 1), high)
    grads_c, grads_c_two, grads_d = (
        together[:, :edge], together[:, edge:far_edge], together[:, far_edge:]
    )

    new_cluster_size = ema_decay * code_usage_average + (1.0 - ema_decay) * counted
    new_embed_sum = jnp.where(
        owner_flag[:, :, None],
        summed * new_cluster_size[:, :, None],
        ema_decay * code_latent_sum_average + (1.0 - ema_decay) * summed,
    )
    new_codebook = new_embed_sum / new_cluster_size[:, :, None]

    def columns(block, at, count):
        return block[:, at * width : (at + count) * width]

    def taps(block):
        return block.reshape(-1, 4, width).transpose(1, 0, 2)

    def unfold(block):
        return block.reshape(-1, 4, width).transpose(1, 0, 2).reshape(-1, width)

    vec = grads_d[:, 3 * width : 3 * width + 16].T
    return (
        output[None],
        activations_grad[None],
        vec[0],
        vec[1],
        columns(grads_d, 0, 3),
        columns(grads_c_two, 4, 1),
        vec[2],
        vec[3],
        vec[4],
        columns(grads_c, 4, 4),
        unfold(columns(grads_c, 0, 4)),
        vec[5],
        taps(columns(grads_c_two, 0, 4)),
        vec[6],
        grads_c_two[:, 5 * width :],
        grads_b[:, 7 * width :].T,
        taps(columns(grads_b, 3, 4)),
        vec[7],
        vec[8],
        vec[9],
        columns(grads_b, 0, 3),
        columns(grads_a, 8, 1),
        vec[10],
        vec[11],
        vec[12],
        columns(grads_a, 4, 4),
        unfold(columns(grads_a, 0, 4)),
        vec[13],
        new_cluster_size,
        new_embed_sum,
        new_codebook,
    )


def solution(mesh):
    grid = mesh.devices
    mesh = jax.sharding.Mesh(
        grid.reshape(grid.shape[0] // 2, 2, grid.shape[1] // 2, 2), ("hi", "lo", "x", "core")
    )
    placed = (
        P(DP, SEQ, None),
        P(SEQ),
        P(SEQ),
        P(SEQ, None),
        P(SEQ, None),
        P(SEQ),
        P(SEQ),
        P(SEQ),
        P(SEQ, None),
        P(SEQ, None),
        P(SEQ),
        P(None, SEQ, None),
        P(SEQ),
        P(SEQ, None),
        P(None, SEQ, None),
        P(None, SEQ),
        P(None, SEQ, None),
        P(SEQ),
        P(SEQ),
        P(SEQ),
        P(SEQ, None),
        P(SEQ, None),
        P(SEQ),
        P(SEQ),
        P(SEQ),
        P(SEQ, None),
        P(SEQ, None),
        P(SEQ),
        P(DP, SEQ, None),
        P(DP, None),
        P(DP, SEQ, None),
        P(),
        P(),
        P(None, DP + SEQ),
        P(None, DP + SEQ, None),
    )
    return jax.shard_map(
        local,
        mesh=mesh,
        in_specs=placed,
        out_specs=(
            P(DP, SEQ, None),
            P(DP, SEQ, None),
            P(DP + SEQ),
            P(DP + SEQ),
            P(DP + SEQ, None),
            P(DP + SEQ, None),
            P(DP + SEQ),
            P(DP + SEQ),
            P(DP + SEQ),
            P(DP + SEQ, None),
            P(DP + SEQ, None),
            P(DP + SEQ),
            P(None, DP + SEQ, None),
            P(DP + SEQ),
            P(DP + SEQ, None),
            P(None, DP + SEQ),
            P(None, DP + SEQ, None),
            P(DP + SEQ),
            P(DP + SEQ),
            P(DP + SEQ),
            P(DP + SEQ, None),
            P(DP + SEQ, None),
            P(DP + SEQ),
            P(DP + SEQ),
            P(DP + SEQ),
            P(DP + SEQ, None),
            P(DP + SEQ, None),
            P(DP + SEQ),
            P(None, DP + SEQ),
            P(None, DP + SEQ, None),
            P(None, DP + SEQ, None),
        ),
        check_vma=False,
    )
```

profile of v0, /device:TPU:0, one launch (start us, length us, event | category | flops | bytes accessed | tf_op | source)
XLA Modules:
  0.0 317.1 jit_solution(15603527231530894571)
XLA Ops:
  7.0 6.5 %all-gather.1 = f32[4,1,3328]{2,1,0:T(1,128)S(1)} all-gather(f32[1,1,3328]{2,1,0:T(1,128)S(1)} %reshape.240), channel_id=2, replica_groups=mesh['hi'=4,'lo'=2,'x'=2,'core'=2] {'x','core'}, dimensions={0}, use_global_device_ids=true | all-gather | bytes 66560 | tf_op jit(solution)/shard_map/all_gather | solution.py:897
  17.8 3.2 %lookup_kernel.1 = (f32[2,304,256]{2,1,0:T(8,128)}, f32[2,304,256]{2,1,0:T(8,128)S(1)}, bf16[2,8,160,256]{3,2,1,0:T(8,128)(2,1)S(1)}, bf16[2,8,160,256]{3,2,1,0:T(8,128)(2,1)S(1)}) custom-call(s32[18]{0:T(128)S(1)} %stack.111.sc_ref, s32[640,8]{1,0:T(8,128)S(1)} %bitcast.175, bf16[8,512,256]{2,1,0:T(8,128)(2,1)S(1)} %copy-done.8), custom_call_target="tpu_custom_call" | custom-call | flops 4000000 | bytes 1 | tf_op jit(solution)/shard_map/lookup_kernel/pallas_call | solution.py:671
  30.4 7.3 %collective-permute-done = bf16[64,3840]{1,0:T(8,128)(2,1)} collective-permute-done((bf16[64,3840]{1,0:T(8,128)(2,1)}, bf16[64,3840]{1,0:T(8,128)(2,1)}, u32[]{:S(2)}, u32[]{:S(2)}) %collective-permute-start) | collective-permute-done | bytes 491552 | tf_op jit(solution)/shard_map/ppermute | solution.py:743
  60.9 7.8 %decoder_front_kernel.1 = (f32[320,512]{1,0:T(8,128)S(1)}, bf16[176,512]{1,0:T(8,128)(2,1)S(1)}, bf16[320,512]{1,0:T(8,128)(2,1)S(1)}, bf16[320,512]{1,0:T(8,128...) custom-call(s32[18]{0:T(128)S(1)} %stack.111.sc_ref, ...), custom_call_target="tpu_custom_call" | custom-call | flops 8000000 | bytes 1 | tf_op jit(solution)/shard_map/decoder_front_kernel/pallas_call | solution.py:671
  68.7 5.5 %collective-permute-done.9 = bf16[64,4352]{1,0:T(8,128)(2,1)S(1)} collective-permute-done((bf16[64,4352]{1,0:T(8,128)(2,1)}, bf16[64,4352]{1,0:T(8,128)(2,1)S(1)}, u32[]{:S(2)}, u32[]{:S(2)}) %collective-permute-start.9) | collective-permute-done | bytes 557088 | tf_op jit(solution)/shard_map/ppermute | solution.py:743
  79.8 13.2 %decoder_layer_kernel.1 = (bf16[320,512]{1,0:T(8,128)(2,1)}, bf16[320,512]{1,0:T(8,128)(2,1)S(1)}, bf16[320,2048]{1,0:T(8,128)(2,1)S(1)}, f32[320,512]{1,0:T(8,1...) custom-call(s32[18]{0:T(128)S(1)} %stack.111.sc_ref, ...), custom_call_target="tpu_custom_call" | custom-call | flops 14000000 | bytes 1 | tf_op jit(solution)/shard_map/decoder_layer_kernel/pallas_call | solution.py:671
  94.8 3.2 %decoder_gradients_kernel.1 = (bf16[256,4608]{1,0:T(8,128)(2,1)S(1)}, bf16[256,4608]{1,0:T(8,128)(2,1)S(1)}) custom-call(s32[18]{0:T(128)S(1)} %stack.111.sc_ref, bf16[320,512]{1,0:T(8,128)(2,1)S(1)} %get-tuple-element.228.n2_ref, bf16[320,2048]{1,0:T(8,128)(2,1)S(1)} %get-tuple-element.229.active_ref, bf16[320,2048]{1,0:T(8,128)(2,1)S(1)} %get-tuple-element.230.dh_ref, ...), custom_call_target="tpu_custom_call" | custom-call | flops 5000000 | bytes 1 | tf_op jit(solution)/shard_map/decoder_gradients_kernel/pallas_call | solution.py:671
  100.9 2.5 collective-permute-start.20
  103.5 3.2 %decoder_back_kernel.1 = (bf16[320,512]{1,0:T(8,128)(2,1)S(1)}, bf16[320,1536]{1,0:T(8,128)(2,1)S(1)}, f32[8,512]{1,0:T(8,128)S(1)}) custom-call(s32[18]{0:T(128)S(1)} %stack.111.sc_ref, bf16[128,3840]{1,0:T(8,128)(2,1)S(1)} %pad_maximum_fusion.5.refs_0_, bf16[128,3840]{1,0:T(8,128)(2,1)S(1)} %pad_maximum_fusion.6.refs_1_, bf16[128,3840]{1,0:T(8,128)(2,1)S(1)} %copy-done.1, ...), custom_call_target="tpu_custom_call" | custom-call | flops 4000000 | bytes 1 | tf_op jit(solution)/shard_map/decoder_back_kernel/pallas_call | solution.py:671
  106.7 11.6 %collective-permute-done.20 = bf16[8,160,256]{2,1,0:T(8,128)(2,1)S(1)} collective-permute-done((bf16[8,160,256]{2,1,0:T(8,128)(2,1)S(1)}, bf16[8,160,256]{2,1,0:T(8,128)(2,1)S(1)}, u32[]{:S(2)}, u32[]{:S(2)}) %collective-permute-start.20) | collective-permute-done | bytes 655392 | tf_op jit(solution)/shard_map/ppermute | solution.py:698
  122.3 5.5 %encoder_front_kernel.1 = (bf16[320,512]{1,0:T(8,128)(2,1)S(1)}, bf16[336,512]{1,0:T(8,128)(2,1)S(1)}, bf16[576,512]{1,0:T(8,128)(2,1)S(1)}, bf16[576,512]{1,0:T(8,128)(2,1)S(1)}, bf16[336,512]{1,0:T(8,128)(2,1)S(1)}) custom-call(s32[18]{0:T(128)S(1)} %stack.111.sc_ref, bf16[128,4352]{1,0:T(8,128)(2,1)S(1)} %constant_dynamic-update-slice_fusion.3.refs_0_.refs_4_, ...), custom_call_target="tpu_custom_call" | custom-call | flops 7000000 | bytes 1 | tf_op jit(solution)/shard_map/encoder_front_kernel/pallas_call | solution.py:671
  127.8 5.2 %middle_kernel.1 = (f32[320,512]{1,0:T(8,128)S(1)}, bf16[160,512]{1,0:T(8,128)(2,1)S(1)}, bf16[160,256]{1,0:T(8,128)(2,1)S(1)}, f32[8,512]{1,0:T(8,128)S(1)}, bf...) custom-call(s32[18]{0:T(128)S(1)} %stack.111.sc_ref, bf16[128,3840]{1,0:T(8,128)(2,1)S(1)} %pad_maximum_fusion.5.refs_0_, ...), custom_call_target="tpu_custom_call" | custom-call | flops 7000000 | bytes 1 | tf_op jit(solution)/shard_map/middle_kernel/pallas_call | solution.py:671
  134.2 5.7 %encoder_forward_kernel.1 = (bf16[336,512]{1,0:T(8,128)(2,1)S(1)}, bf16[320,512]{1,0:T(8,128)(2,1)S(1)}, bf16[320,2048]{1,0:T(8,128)(2,1)S(1)}, f32[320,2048]{1,...) custom-call(s32[18]{0:T(128)S(1)} %stack.111.sc_ref, ...), custom_call_target="tpu_custom_call" | custom-call | flops 6000000 | bytes 1 | tf_op jit(solution)/shard_map/encoder_forward_kernel/pallas_call | solution.py:671
  140.0 7.7 %collective-permute-done.25 = bf16[128,4608]{1,0:T(8,128)(2,1)S(1)} collective-permute-done((bf16[128,4608]{1,0:T(8,128)(2,1)S(1)}, bf16[128,4608]{1,0:T(8,128)(2,1)S(1)}, u32[]{:S(2)}, u32[]{:S(2)}) %collective-permute-start.25) | collective-permute-done | bytes 1179680 | tf_op jit(solution)/shard_map/ppermute | solution.py:698
  151.3 2.5 collective-permute-start.26
  154.1 8.2 %encoder_backward_kernel.1 = (f32[320,512]{1,0:T(8,128)S(1)}, bf16[320,2048]{1,0:T(8,128)(2,1)S(1)}, bf16[320,512]{1,0:T(8,128)(2,1)S(1)}, bf16[320,512]{1,0:T(8...) custom-call(s32[18]{0:T(128)S(1)} %stack.111.sc_ref, ...), custom_call_target="tpu_custom_call" | custom-call | flops 11000000 | bytes 1 | tf_op jit(solution)/shard_map/encoder_backward_kernel/pallas_call | solution.py:671
  163.5 5.9 %collective-permute-done.26.x_ref = bf16[8,160,256]{2,1,0:T(8,128)(2,1)S(1)} collective-permute-done((bf16[8,160,256]{2,1,0:T(8,128)(2,1)S(1)}, bf16[8,160,256]{2,1,0:T(8,128)(2,1)S(1)}, u32[]{:S(2)}, u32[]{:S(2)}) %collective-permute-start.26) | collective-permute-done | bytes 655392 | tf_op jit(solution)/shard_map/ppermute | solution.py:743
  171.7 6.3 %collect_kernel.1 = (bf16[4,528,256]{2,1,0:T(8,128)(2,1)}, bf16[4,528,256]{2,1,0:T(8,128)(2,1)S(1)}) custom-call(s32[18]{0:T(128)S(1)} %stack.111.sc_ref, bf16[8,160,256]{2,1,0:T(8,128)(2,1)S(1)} %get-tuple-element.266.own_ref, bf16[8,160,256]{2,1,0:T(8,128)(2,1)S(1)} %collective-permute-done.26.x_ref, ...), custom_call_target="tpu_custom_call" | custom-call | flops 5000000 | bytes 1 | tf_op jit(solution)/shard_map/collect_kernel/pallas_call | solution.py:671
  178.1 3.8 %encoder_gradients_kernel.1 = (bf16[256,4096]{1,0:T(8,128)(2,1)S(1)}, bf16[256,4096]{1,0:T(8,128)(2,1)S(1)}, bf16[256,2816]{1,0:T(8,128)(2,1)S(1)}, bf16[256,2816]{1,0:T(8,128)(2,1)S(1)}) custom-call(s32[18]{0:T(128)S(1)} %stack.111.sc_ref, bf16[320,512]{1,0:T(8,128)(2,1)S(1)} %get-tuple-element.285.n2_ref, ...), custom_call_target="tpu_custom_call" | custom-call | flops 5000000 | bytes 1 | tf_op jit(solution)/shard_map/encoder_gradients_kernel/pallas_call | solution.py:671
  181.9 8.3 %collective-permute-start.32 = (bf16[256,2816]{1,0:T(8,128)(2,1)S(1)}, bf16[256,2816]{1,0:T(8,128)(2,1)S(1)}, u32[]{:S(2)}, u32[]{:S(2)}) collective-permute-start(bf16[256,2816]{1,0:T(8,128)(2,1)S(1)} %get-tuple-element.302), channel_id=1, source_target_pairs={{0,1},{1,0},{2,3},{3,2},{4,5},{5,4},{6,7},{7,6},{8,9},{9,8},{10,11... | collective-permute-start | bytes 4325384 | tf_op jit(solution)/shard_map/ppermute | solution.py:719
  193.4 2.6 collective-permute-done.31
  196.8 3.5 %encoder_back_kernel.1 = (bf16[320,512]{1,0:T(8,128)(2,1)}, bf16[256,1664]{1,0:T(8,128)(2,1)S(1)}, bf16[256,1664]{1,0:T(8,128)(2,1)S(1)}) custom-call(s32[18]{0:T(128)S(1)} %stack.111.sc_ref, bf16[128,4352]{1,0:T(8,128)(2,1)S(1)} %constant_dynamic-update-slice_fusion.3.refs_0_.refs_4_, bf16[128,4352]{1,0:T(8,128)(2,1)S(1)} %pad_maximum_fusion.1.refs_1_.refs_5_, ...), custom_call_target="tpu_custom_call" | custom-call | flops 5000000 | bytes 1 | tf_op jit(solution)/shard_map/encoder_back_kernel/pallas_call | solution.py:671
  206.1 8.8 %collective-permute-done.36 = bf16[64,3840]{1,0:T(8,128)(2,1)S(1)} collective-permute-done((bf16[64,3840]{1,0:T(8,128)(2,1)S(1)}, bf16[64,3840]{1,0:T(8,128)(2,1)S(1)}, u32[]{:S(2)}, u32[]{:S(2)}) %collective-permute-start.36) | collective-permute-done | bytes 491552 | tf_op jit(solution)/shard_map/ppermute | solution.py:698
  216.2 4.9 %all-to-all-start.1 = ((bf16[4,16,8448]{2,1,0:T(8,128)(2,1)}), bf16[4,16,8448]{2,1,0:T(8,128)(2,1)S(1)}, u32[]{:S(2)}, u32[]{:S(2)}) async-start(bf16[4,16,8448]{2,1,0:T(8,128)(2,1)} %bitcast.88), calls=%async_computation.1 | async-start | bytes 2162688 | tf_op jit(solution)/shard_map/all_to_all | solution.py:726
  222.1 2.7 add_convert_fusion.5
  224.8 11.9 %collective-permute-done.34 = bf16[128,4096]{1,0:T(8,128)(2,1)} collective-permute-done((bf16[128,4096]{1,0:T(8,128)(2,1)}, bf16[128,4096]{1,0:T(8,128)(2,1)}, u32[]{:S(2)}, u32[]{:S(2)}) %collective-permute-start.34) | collective-permute-done | bytes 1048608 | tf_op jit(solution)/shard_map/ppermute | solution.py:698
  243.0 9.1 %collective-permute-done.42 = bf16[64,2816]{1,0:T(8,128)(2,1)S(1)} collective-permute-done((bf16[64,2816]{1,0:T(8,128)(2,1)S(1)}, bf16[64,2816]{1,0:T(8,128)(2,1)S(1)}, u32[]{:S(2)}, u32[]{:S(2)}) %collective-permute-start.42) | collective-permute-done | bytes 360480 | tf_op jit(solution)/shard_map/ppermute | solution.py:698
  252.1 2.5 collective-permute-done.41
  255.9 4.8 %all-to-all-start = ((bf16[4,16,8576]{2,1,0:T(8,128)(2,1)}), bf16[4,16,8576]{2,1,0:T(8,128)(2,1)S(1)}, u32[]{:S(2)}, u32[]{:S(2)}) async-start(bf16[4,16,8576]{2,1,0:T(8,128)(2,1)} %bitcast.83), calls=%async_computation | async-start | bytes 2195456 | tf_op jit(solution)/shard_map/all_to_all | solution.py:726
  262.2 23.6 %all-to-all-done = bf16[4,16,8576]{2,1,0:T(8,128)(2,1)S(1)} async-done(((bf16[4,16,8576]{2,1,0:T(8,128)(2,1)}), bf16[4,16,8576]{2,1,0:T(8,128)(2,1)S(1)}, u32[]{:S(2)}, u32[]{:S(2)}) %all-to-all-start) | async-done | bytes 1097760 | tf_op jit(solution)/shard_map/all_to_all | solution.py:726
  285.8 3.5 %all-to-all-start.2 = ((bf16[4,528,256]{2,1,0:T(8,128)(2,1)}), bf16[4,528,256]{2,1,0:T(8,128)(2,1)S(1)}, u32[]{:S(2)}, u32[]{:S(2)}) async-start(bf16[4,528,256]{2,1,0:T(8,128)(2,1)} %add_convert_fusion.5), calls=%async_computation.2 | async-start | bytes 2162688 | tf_op jit(solution)/shard_map/all_to_all | solution.py:726
  297.0 18.2 %all-to-all-done.2 = bf16[4,528,256]{2,1,0:T(8,128)(2,1)S(1)} async-done(((bf16[4,528,256]{2,1,0:T(8,128)(2,1)}), bf16[4,528,256]{2,1,0:T(8,128)(2,1)S(1)}, u32[]{:S(2)}, u32[]{:S(2)}) %all-to-all-start.2) | async-done | bytes 1081376 | tf_op jit(solution)/shard_map/all_to_all | solution.py:726
  (290 shorter events, 95.1 us)
Async XLA Ops:
  3.1 12.6 %collective-permute-start.2 = (bf16[128,3840]{1,0:T(8,128)(2,1)S(1)}, bf16[128,3840]{1,0:T(8,128)(2,1)S(1)}, u32[]{:S(2)}, u32[]{:S(2)}) collective-permute-start(bf16[128,3840]{1,0:T(8,128)(2,1)S(1)} %pad_maximum_fusion.5.refs_0_), channel_id=1, source_target_pairs={{0,1},{1,0},{2,3},{3,2},{4,5},{5,4},{6,7},{7,6},{8,9},{9,8},{10,11... | collective-permute-start | bytes 2949128 | tf_op jit(solution)/shard_map/ppermute | solution.py:743
  23.3 14.4 %collective-permute-start = (bf16[64,3840]{1,0:T(8,128)(2,1)}, bf16[64,3840]{1,0:T(8,128)(2,1)}, u32[]{:S(2)}, u32[]{:S(2)}) collective-permute-start(bf16[64,3840]{1,0:T(8,128)(2,1)} %constant_dynamic-slice_fusion.5), channel_id=1, source_target_pairs={{0,2},{2,0},{1,3},{3,1},{4,6},{6,4},{5,7},{7,5},{8,10},{10,8},{9,1... | collective-permute-start | bytes 1474568 | tf_op jit(solution)/shard_map/ppermute | solution.py:743
  30.2 26.3 %collective-permute-start.4 = (f32[304,256]{1,0:T(8,128)}, f32[304,256]{1,0:T(8,128)}, u32[]{:S(2)}, u32[]{:S(2)}) collective-permute-start(f32[304,256]{1,0:T(8,128)} %dynamic-slice_bitcast_fusion.10), channel_id=1, source_target_pairs={{0,2},{2,0},{1,3},{3,1},{4,6},{6,4},{5,7},{7,5},{8,10},{10,8},{9,1... | collective-permute-start | bytes 933896 | tf_op jit(solution)/shard_map/ppermute | solution.py:743
  43.7 13.9 %collective-permute-start.5 = (bf16[64,4608]{1,0:T(8,128)(2,1)}, bf16[64,4608]{1,0:T(8,128)(2,1)}, u32[]{:S(2)}, u32[]{:S(2)}) collective-permute-start(bf16[64,4608]{1,0:T(8,128)(2,1)} %constant_dynamic-slice_fusion.4), channel_id=1, source_target_pairs={{0,2},{2,0},{1,3},{3,1},{4,6},{6,4},{5,7},{7,5},{8,10},{10,8},{9,1... | collective-permute-start | bytes 1769480 | tf_op jit(solution)/shard_map/ppermute | solution.py:743
  57.6 16.6 %collective-permute-start.8 = (bf16[64,4608]{1,0:T(8,128)(2,1)}, bf16[64,4608]{1,0:T(8,128)(2,1)S(1)}, u32[]{:S(2)}, u32[]{:S(2)}) collective-permute-start(bf16[64,4608]{1,0:T(8,128)(2,1)} %collective-permute-done.5), channel_id=1, source_target_pairs={{0,4},{4,0},{1,5},{5,1},{2,6},{6,2},{3,7},{7,3},{8,12},{12,8},{9,1... | collective-permute-start | bytes 1769480 | tf_op jit(solution)/shard_map/ppermute | solution.py:743
  59.3 14.9 %collective-permute-start.9 = (bf16[64,4352]{1,0:T(8,128)(2,1)}, bf16[64,4352]{1,0:T(8,128)(2,1)S(1)}, u32[]{:S(2)}, u32[]{:S(2)}) collective-permute-start(bf16[64,4352]{1,0:T(8,128)(2,1)} %constant_dynamic-slice_fusion.3), channel_id=1, source_target_pairs={{0,2},{2,0},{1,3},{3,1},{4,6},{6,4},{5,7},{7,5},{8,10},{10,8},{9,1... | collective-permute-start | bytes 1671176 | tf_op jit(solution)/shard_map/ppermute | solution.py:743
  60.8 19.0 %collective-permute-start.10 = (bf16[128,4608]{1,0:T(8,128)(2,1)S(1)}, bf16[128,4608]{1,0:T(8,128)(2,1)S(1)}, u32[]{:S(2)}, u32[]{:S(2)}) collective-permute-start(bf16[128,4608]{1,0:T(8,128)(2,1)S(1)} %copy-done.6), channel_id=1, source_target_pairs={{0,1},{1,0},{2,3},{3,2},{4,5},{5,4},{6,7},{7,6},{8,9},{9,8},{10,11... | collective-permute-start | bytes 3538952 | tf_op jit(solution)/shard_map/ppermute | solution.py:743
  74.2 20.1 %collective-permute-start.14 = (bf16[2,8,160,256]{3,2,1,0:T(8,128)(2,1)S(1)}, bf16[2,8,160,256]{3,2,1,0:T(8,128)(2,1)S(1)}, u32[]{:S(2)}, u32[]{:S(2)}) collective-permute-start(bf16[2,8,160,256]{3,2,1,0:T(8,128)(2,1)S(1)} %copy-done.16), channel_id=1, source_target_pairs={{0,1},{1,0},{2,3},{3,2},{4,5},{5,4},{6,7},{7,6},{8,9},{9,8},{10,11... | collective-permute-start | bytes 3932168 | tf_op jit(solution)/shard_map/ppermute | solution.py:719
  77.1 17.7 %collective-permute-start.12 = (bf16[64,4352]{1,0:T(8,128)(2,1)S(1)}, bf16[64,4352]{1,0:T(8,128)(2,1)S(1)}, u32[]{:S(2)}, u32[]{:S(2)}) collective-permute-start(bf16[64,4352]{1,0:T(8,128)(2,1)S(1)} %collective-permute-done.9), channel_id=1, source_target_pairs={{0,4},{4,0},{1,5},{5,1},{2,6},{6,2},{3,7},{7,3},{8,12},{12,8},{9,1... | collective-permute-start | bytes 1671176 | tf_op jit(solution)/shard_map/ppermute | solution.py:743
  78.2 16.6 %collective-permute-start.13 = (bf16[64,4096]{1,0:T(8,128)(2,1)S(1)}, bf16[64,4096]{1,0:T(8,128)(2,1)S(1)}, u32[]{:S(2)}, u32[]{:S(2)}) collective-permute-start(bf16[64,4096]{1,0:T(8,128)(2,1)S(1)} %constant_dynamic-slice_fusion), channel_id=1, source_target_pairs={{0,2},{2,0},{1,3},{3,1},{4,6},{6,4},{5,7},{7,5},{8,10},{10,8},{9,1... | collective-permute-start | bytes 1572872 | tf_op jit(solution)/shard_map/ppermute | solution.py:743
  98.0 20.9 %collective-permute-start.17 = (bf16[256,4608]{1,0:T(8,128)(2,1)S(1)}, bf16[256,4608]{1,0:T(8,128)(2,1)S(1)}, u32[]{:S(2)}, u32[]{:S(2)}) collective-permute-start(bf16[256,4608]{1,0:T(8,128)(2,1)S(1)} %get-tuple-element.236), channel_id=1, source_target_pairs={{0,1},{1,0},{2,3},{3,2},{4,5},{5,4},{6,7},{7,6},{8,9},{9,8},{10,11... | collective-permute-start | bytes 7077896 | tf_op jit(solution)/shard_map/ppermute | solution.py:719
  99.2 21.8 %collective-permute-start.15 = (bf16[128,4352]{1,0:T(8,128)(2,1)S(1)}, bf16[128,4352]{1,0:T(8,128)(2,1)S(1)}, u32[]{:S(2)}, u32[]{:S(2)}) collective-permute-start(bf16[128,4352]{1,0:T(8,128)(2,1)S(1)} %constant_dynamic-update-slice_fusion.3.refs_0_.refs_4_), channel_id=1, source_target_pairs={{0,1},{1,0},{2,3},{3,2},{4,5},{5,4},{6,7},{7,6},{8,9},{9,8},{10,11... | collective-permute-start | bytes 3342344 | tf_op jit(solution)/shard_map/ppermute | solution.py:743
  99.3 34.9 %collective-permute-start.21 = (bf16[128,4096]{1,0:T(8,128)(2,1)S(1)}, bf16[128,4096]{1,0:T(8,128)(2,1)S(1)}, u32[]{:S(2)}, u32[]{:S(2)}) collective-permute-start(bf16[128,4096]{1,0:T(8,128)(2,1)S(1)} %constant_dynamic-update-slice_fusion.7.refs_4_), channel_id=1, source_target_pairs={{0,1},{1,0},{2,3},{3,2},{4,5},{5,4},{6,7},{7,6},{8,9},{9,8},{10,11... | collective-permute-start | bytes 3145736 | tf_op jit(solution)/shard_map/ppermute | solution.py:743
  99.7 19.8 %collective-permute-start.19 = (bf16[64,4096]{1,0:T(8,128)(2,1)S(1)}, bf16[64,4096]{1,0:T(8,128)(2,1)S(1)}, u32[]{:S(2)}, u32[]{:S(2)}) collective-permute-start(bf16[64,4096]{1,0:T(8,128)(2,1)S(1)} %collective-permute-done.13), channel_id=1, source_target_pairs={{0,4},{4,0},{1,5},{5,1},{2,6},{6,2},{3,7},{7,3},{8,12},{12,8},{9,1... | collective-permute-start | bytes 1572872 | tf_op jit(solution)/shard_map/ppermute | solution.py:743
  100.9 17.5 %collective-permute-start.20 = (bf16[8,160,256]{2,1,0:T(8,128)(2,1)S(1)}, bf16[8,160,256]{2,1,0:T(8,128)(2,1)S(1)}, u32[]{:S(2)}, u32[]{:S(2)}) collective-permute-start(bf16[8,160,256]{2,1,0:T(8,128)(2,1)S(1)} %dynamic-slice_bitcast_fusion.4), channel_id=1, source_target_pairs={{0,2},{2,0},{1,3},{3,1},{4,6},{6,4},{5,7},{7,5},{8,10},{10,8},{9,1... | collective-permute-start | bytes 1966088 | tf_op jit(solution)/shard_map/ppermute | solution.py:698
  119.6 28.1 %collective-permute-start.25 = (bf16[128,4608]{1,0:T(8,128)(2,1)S(1)}, bf16[128,4608]{1,0:T(8,128)(2,1)S(1)}, u32[]{:S(2)}, u32[]{:S(2)}) collective-permute-start(bf16[128,4608]{1,0:T(8,128)(2,1)S(1)} %dynamic-slice_bitcast_fusion), channel_id=1, source_target_pairs={{0,4},{4,0},{1,5},{5,1},{2,6},{6,2},{3,7},{7,3},{8,12},{12,8},{9,1... | collective-permute-start | bytes 3538952 | tf_op jit(solution)/shard_map/ppermute | solution.py:698
  120.9 13.3 %collective-permute-start.22 = (bf16[128,4096]{1,0:T(8,128)(2,1)S(1)}, bf16[128,4096]{1,0:T(8,128)(2,1)S(1)}, u32[]{:S(2)}, u32[]{:S(2)}) collective-permute-start(bf16[128,4096]{1,0:T(8,128)(2,1)S(1)} %pad_maximum_fusion.4.refs_5_), channel_id=1, source_target_pairs={{0,1},{1,0},{2,3},{3,2},{4,5},{5,4},{6,7},{7,6},{8,9},{9,8},{10,11... | collective-permute-start | bytes 3145736 | tf_op jit(solution)/shard_map/ppermute | solution.py:743
  133.0 14.9 %collective-permute-start.24 = (bf16[256,3840]{1,0:T(8,128)(2,1)S(1)}, bf16[256,3840]{1,0:T(8,128)(2,1)S(1)}, u32[]{:S(2)}, u32[]{:S(2)}) collective-permute-start(bf16[256,3840]{1,0:T(8,128)(2,1)S(1)} %get-tuple-element.261), channel_id=1, source_target_pairs={{0,1},{1,0},{2,3},{3,2},{4,5},{5,4},{6,7},{7,6},{8,9},{9,8},{10,11... | collective-permute-start | bytes 5898248 | tf_op jit(solution)/shard_map/ppermute | solution.py:719
  148.5 23.0 %collective-permute-start.29 = (bf16[128,3840]{1,0:T(8,128)(2,1)S(1)}, bf16[128,3840]{1,0:T(8,128)(2,1)S(1)}, u32[]{:S(2)}, u32[]{:S(2)}) collective-permute-start(bf16[128,3840]{1,0:T(8,128)(2,1)S(1)} %dynamic-slice_bitcast_fusion.2), channel_id=1, source_target_pairs={{0,4},{4,0},{1,5},{5,1},{2,6},{6,2},{3,7},{7,3},{8,12},{12,8},{9,1... | collective-permute-start | bytes 2949128 | tf_op jit(solution)/shard_map/ppermute | solution.py:698
  151.3 18.2 %collective-permute-start.26 = (bf16[8,160,256]{2,1,0:T(8,128)(2,1)S(1)}, bf16[8,160,256]{2,1,0:T(8,128)(2,1)S(1)}, u32[]{:S(2)}, u32[]{:S(2)}) collective-permute-start(bf16[8,160,256]{2,1,0:T(8,128)(2,1)S(1)} %get-tuple-element.266.own_ref), channel_id=1, source_target_pairs={{0,2},{2,0},{1,3},{3,1},{4,6},{6,4},{5,7},{7,5},{8,10},{10,8},{9,1... | collective-permute-start | bytes 1966088 | tf_op jit(solution)/shard_map/ppermute | solution.py:743
  153.8 15.6 %collective-permute-start.27 = (bf16[8,160,256]{2,1,0:T(8,128)(2,1)S(1)}, bf16[8,160,256]{2,1,0:T(8,128)(2,1)S(1)}, u32[]{:S(2)}, u32[]{:S(2)}) collective-permute-start(bf16[8,160,256]{2,1,0:T(8,128)(2,1)S(1)} %get-tuple-element.266.own_ref), channel_id=1, source_target_pairs={{0,1},{1,0},{2,3},{3,2},{4,5},{5,4},{6,7},{7,6},{8,9},{9,8},{10,11... | collective-permute-start | bytes 1966088 | tf_op jit(solution)/shard_map/ppermute | solution.py:743
  153.9 36.4 %collective-permute-start.33 = (bf16[64,4608]{1,0:T(8,128)(2,1)S(1)}, bf16[64,4608]{1,0:T(8,128)(2,1)S(1)}, u32[]{:S(2)}, u32[]{:S(2)}) collective-permute-start(bf16[64,4608]{1,0:T(8,128)(2,1)S(1)} %dynamic-slice_bitcast_fusion.5), channel_id=1, source_target_pairs={{0,2},{2,0},{1,3},{3,1},{4,6},{6,4},{5,7},{7,5},{8,10},{10,8},{9,1... | collective-permute-start | bytes 1769480 | tf_op jit(solution)/shard_map/ppermute | solution.py:698
  162.2 15.8 %collective-permute-start.30 = (bf16[256,1024]{1,0:T(8,128)(2,1)S(1)}, bf16[256,1024]{1,0:T(8,128)(2,1)S(1)}, u32[]{:S(2)}, u32[]{:S(2)}) collective-permute-start(bf16[256,1024]{1,0:T(8,128)(2,1)S(1)} %get-tuple-element.284), channel_id=1, source_target_pairs={{1,0},{2,1},{3,2},{5,4},{6,5},{7,6},{9,8},{10,9},{11,10},{13,12},{... | collective-permute-start | bytes 1572872 | tf_op jit(solution)/shard_map/ppermute | solution.py:733
  190.4 30.6 %collective-permute-start.35 = (bf16[4,528,256]{2,1,0:T(8,128)(2,1)}, bf16[4,528,256]{2,1,0:T(8,128)(2,1)}, u32[]{:S(2)}, u32[]{:S(2)}) collective-permute-start(bf16[4,528,256]{2,1,0:T(8,128)(2,1)} %get-tuple-element.318), channel_id=1, source_target_pairs={{0,4},{4,0},{1,5},{5,1},{2,6},{6,2},{3,7},{7,3},{8,12},{12,8},{9,1... | collective-permute-start | bytes 3244040 | tf_op jit(solution)/shard_map/ppermute | solution.py:719
  200.8 14.1 %collective-permute-start.36 = (bf16[64,3840]{1,0:T(8,128)(2,1)S(1)}, bf16[64,3840]{1,0:T(8,128)(2,1)S(1)}, u32[]{:S(2)}, u32[]{:S(2)}) collective-permute-start(bf16[64,3840]{1,0:T(8,128)(2,1)S(1)} %dynamic-slice_bitcast_fusion.7), channel_id=1, source_target_pairs={{0,2},{2,0},{1,3},{3,1},{4,6},{6,4},{5,7},{7,5},{8,10},{10,8},{9,1... | collective-permute-start | bytes 1474568 | tf_op jit(solution)/shard_map/ppermute | solution.py:698
  202.0 34.7 %collective-permute-start.34 = (bf16[128,4096]{1,0:T(8,128)(2,1)}, bf16[128,4096]{1,0:T(8,128)(2,1)}, u32[]{:S(2)}, u32[]{:S(2)}) collective-permute-start(bf16[128,4096]{1,0:T(8,128)(2,1)} %dynamic-slice_bitcast_fusion.1), channel_id=1, source_target_pairs={{0,2},{2,0},{1,3},{3,1},{4,6},{6,4},{5,7},{7,5},{8,10},{10,8},{9,1... | collective-permute-start | bytes 3145736 | tf_op jit(solution)/shard_map/ppermute | solution.py:698
  204.9 34.4 %collective-permute-start.40 = (bf16[128,2816]{1,0:T(8,128)(2,1)}, bf16[128,2816]{1,0:T(8,128)(2,1)}, u32[]{:S(2)}, u32[]{:S(2)}) collective-permute-start(bf16[128,2816]{1,0:T(8,128)(2,1)} %dynamic-slice_bitcast_fusion.3), channel_id=1, source_target_pairs={{0,4},{4,0},{1,5},{5,1},{2,6},{6,2},{3,7},{7,3},{8,12},{12,8},{9,1... | collective-permute-start | bytes 2162696 | tf_op jit(solution)/shard_map/ppermute | solution.py:698
  216.2 39.8 %all-to-all-start.1 = ((bf16[4,16,8448]{2,1,0:T(8,128)(2,1)}), bf16[4,16,8448]{2,1,0:T(8,128)(2,1)S(1)}, u32[]{:S(2)}, u32[]{:S(2)}) async-start(bf16[4,16,8448]{2,1,0:T(8,128)(2,1)} %bitcast.88), calls=%async_computation.1 | async-start | bytes 2162688 | tf_op jit(solution)/shard_map/all_to_all | solution.py:726
  221.1 20.9 %collective-permute-start.39 = (bf16[128,1664]{1,0:T(8,128)(2,1)S(1)}, bf16[128,1664]{1,0:T(8,128)(2,1)S(1)}, u32[]{:S(2)}, u32[]{:S(2)}) collective-permute-start(bf16[128,1664]{1,0:T(8,128)(2,1)S(1)} %dynamic-slice_bitcast_fusion.8), channel_id=1, source_target_pairs={{0,4},{4,0},{1,5},{5,1},{2,6},{6,2},{3,7},{7,3},{8,12},{12,8},{9,1... | collective-permute-start | bytes 1277960 | tf_op jit(solution)/shard_map/ppermute | solution.py:698
  238.3 16.4 %collective-permute-start.38 = (bf16[64,4096]{1,0:T(8,128)(2,1)S(1)}, bf16[64,4096]{1,0:T(8,128)(2,1)S(1)}, u32[]{:S(2)}, u32[]{:S(2)}) collective-permute-start(bf16[64,4096]{1,0:T(8,128)(2,1)S(1)} %dynamic-slice_bitcast_fusion.6), channel_id=1, source_target_pairs={{0,4},{4,0},{1,5},{5,1},{2,6},{6,2},{3,7},{7,3},{8,12},{12,8},{9,1... | collective-permute-start | bytes 1572872 | tf_op jit(solution)/shard_map/ppermute | solution.py:698
  255.9 29.9 %all-to-all-start = ((bf16[4,16,8576]{2,1,0:T(8,128)(2,1)}), bf16[4,16,8576]{2,1,0:T(8,128)(2,1)S(1)}, u32[]{:S(2)}, u32[]{:S(2)}) async-start(bf16[4,16,8576]{2,1,0:T(8,128)(2,1)} %bitcast.83), calls=%async_computation | async-start | bytes 2195456 | tf_op jit(solution)/shard_map/all_to_all | solution.py:726
  285.8 29.4 %all-to-all-start.2 = ((bf16[4,528,256]{2,1,0:T(8,128)(2,1)}), bf16[4,528,256]{2,1,0:T(8,128)(2,1)S(1)}, u32[]{:S(2)}, u32[]{:S(2)}) async-start(bf16[4,528,256]{2,1,0:T(8,128)(2,1)} %add_convert_fusion.5), calls=%async_computation.2 | async-start | bytes 2162688 | tf_op jit(solution)/shard_map/all_to_all | solution.py:726
  (66 other events, 448.3 us)
where the time goes:
time: 322 us; the launch traced here: 317 us
  waiting for transfers between devices  120 us (37%)
  Pallas kernels  70.7 us (22%)
  starting transfers between devices  59.6 us (19%)
  local copies, waits for them, and re-layouts  33.1 us (10%)
  other arithmetic  24.5 us (8%)
  blocking collectives  6.47 us (2%)
    pallas_call x13, Pallas kernels, call(): pl.pallas_call(kernel, name=title, out_shape=outs, in_specs=[pl.BlockSpec...  70.7 us
    ppermute x11, waiting for transfers between devices, halve(): got = lax.ppermute(sent, axis, [(0, 1), (1, 0)])  54.6 us
    all_to_all x3, waiting for transfers between devices, sum_over_hi(): parts = lax.all_to_all(block, 'hi', 0, 0, tiled=True)  41.8 us
    ppermute x20, waiting for transfers between devices, swap(): return lax.ppermute(block, axis, [(0, 1), (1, 0)])  19.5 us
    ppermute x20, starting transfers between devices, swap(): return lax.ppermute(block, axis, [(0, 1), (1, 0)])  16.9 us
    all_to_all x3, starting transfers between devices, sum_over_hi(): parts = lax.all_to_all(block, 'hi', 0, 0, tiled=True)  13.2 us
    ppermute x8, starting transfers between devices, swap_add(): got = lax.ppermute(send, axis, [(0, 1), (1, 0)])  12.4 us
    unnamed x117, local copies, waits for them, and re-layouts  12.3 us
  transfers between devices with their start and end apart: 46, of which 16 were waited for; matrix products, arithmetic and copies ran while one was open for 15% of the time, Pallas kernels for 21%

commit v1 on v0

--- a/solution.py
+++ b/solution.py
@@ -1246,8 +1246,7 @@
         combined = swap_add(csend, ckeep, "lo", b_sum)
         c_one = next_sum(c_one, ORDER_C_ONE[0], index, combined)
         together = last_sum(jnp.concatenate([a_sum, b_sum], 1), high)
-        combined, together = tie(combined, together)
-        combined = sum_over_hi(combined)
+        combined = sum_by_permutes(combined, index)
         summed = combined[:tail_rows].reshape(levels, code_share, latent)
         digits = combined[tail_rows:, :code_share]
         counted = 128.0 * digits[:levels] + digits[levels:]
@@ -1270,7 +1269,9 @@
         counted = lax.psum_scatter(counts, DP, scatter_dimension=1, tiled=False)
     c_two = next_sum(c_two, ORDER_C_TWO[0], index, c_one)
     d_sum = next_sum(d_sum, ORDER_D[0], index, c_two)
-    c_two = next_sum(c_two, ORDER_C_TWO[1], index, d_sum)
+    c_two = next_sum(
+        c_two, ORDER_C_TWO[1], index, combined if code_share % 16 == 0 else d_sum
+    )
     d_sum = next_sum(d_sum, ORDER_D[1], index, c_two)
     c_one = next_sum(c_one, ORDER_C_ONE[1], index, d_sum)
     grads_a, grads_b = together[:, : a_sum.shape[1]], together[:, a_sum.shape[1] :]

time: 322 us -> 310 us (0.963)
  waiting for transfers between devices: 120 us -> 104 us
  local copies, waits for them, and re-layouts: 33.1 us -> 37 us
    all_to_all x3 -> x2, waiting for transfers between devices: 41.8 us -> 28.8 us  [sum_over_hi(): parts = lax.all_to_all(block, 'hi', 0, 0, tiled=True)]
    ppermute x11, waiting for transfers between devices: 54.6 us -> 44.8 us  [halve(): got = lax.ppermute(sent, axis, [(0, 1), (1, 0)])]
    ppermute x0 -> x3, waiting for transfers between devices: none -> 5.92 us  [sum_by_permutes(): got = lax.ppermute(sent, 'hi', [(i, i ^ turn) for i in range(count)])]
    all_to_all x3 -> x2, starting transfers between devices: 13.2 us -> 8.75 us  [sum_over_hi(): parts = lax.all_to_all(block, 'hi', 0, 0, tiled=True)]
    ppermute x0 -> x3, starting transfers between devices: none -> 4.39 us  [sum_by_permutes(): got = lax.ppermute(sent, 'hi', [(i, i ^ turn) for i in range(count)])]
    unnamed x117 -> x125, local copies, waits for them, and re-layouts: 12.3 us -> 14.1 us
  transfers between devices with their start and end apart: 46 -> 48, of which waited for: 16 -> 19; matrix products, arithmetic and copies ran while one was open for 15% -> 15% of each run, Pallas kernels for 21% -> 22%
where the time goes in v1:
time: 310 us; the launch traced here: 305 us
  waiting for transfers between devices  104 us (34%)
  Pallas kernels  70.3 us (23%)
  starting transfers between devices  60 us (19%)
  local copies, waits for them, and re-layouts  37 us (12%)
  other arithmetic  24.5 us (8%)
  blocking collectives  6.47 us (2%)
    pallas_call x13, Pallas kernels, call(): pl.pallas_call(kernel, name=title, out_shape=outs, in_specs=[pl.BlockSpec...  70.3 us
    ppermute x11, waiting for transfers between devices, halve(): got = lax.ppermute(sent, axis, [(0, 1), (1, 0)])  44.8 us
    all_to_all x2, waiting for transfers between devices, sum_over_hi(): parts = lax.all_to_all(block, 'hi', 0, 0, tiled=True)  28.8 us
    ppermute x20, waiting for transfers between devices, swap(): return lax.ppermute(block, axis, [(0, 1), (1, 0)])  18.4 us
    ppermute x20, starting transfers between devices, swap(): return lax.ppermute(block, axis, [(0, 1), (1, 0)])  16.9 us
    unnamed x125, local copies, waits for them, and re-layouts  14.1 us
    ppermute x8, starting transfers between devices, swap_add(): got = lax.ppermute(send, axis, [(0, 1), (1, 0)])  13.4 us
    ppermute x11, starting transfers between devices, halve(): got = lax.ppermute(sent, axis, [(0, 1), (1, 0)])  10.7 us
  transfers between devices with their start and end apart: 48, of which 19 were waited for; matrix products, arithmetic and copies ran while one was open for 15% of the time, Pallas kernels for 22%

profile of v1, /device:TPU:0, one launch (start us, length us, event | category | flops | bytes accessed | tf_op | source)
XLA Modules:
  0.0 304.9 jit_solution(11788379512884511406)
XLA Ops:
  7.0 6.5 %all-gather.1 = f32[4,1,3328]{2,1,0:T(1,128)S(1)} all-gather(f32[1,1,3328]{2,1,0:T(1,128)S(1)} %reshape.243), channel_id=2, replica_groups=mesh['hi'=4,'lo'=2,'x'=2,'core'=2] {'x','core'}, dimensions={0}, use_global_device_ids=true | all-gather | bytes 66560 | tf_op jit(solution)/shard_map/all_gather | solution.py:897
  17.8 3.2 %lookup_kernel.1 = (f32[2,304,256]{2,1,0:T(8,128)}, f32[2,304,256]{2,1,0:T(8,128)S(1)}, bf16[2,8,160,256]{3,2,1,0:T(8,128)(2,1)S(1)}, bf16[2,8,160,256]{3,2,1,0:T(8,128)(2,1)S(1)}) custom-call(s32[18]{0:T(128)S(1)} %stack.111.sc_ref, s32[640,8]{1,0:T(8,128)S(1)} %bitcast.184, bf16[8,512,256]{2,1,0:T(8,128)(2,1)S(1)} %copy-done.8), custom_call_target="tpu_custom_call" | custom-call | flops 4000000 | bytes 1 | tf_op jit(solution)/shard_map/lookup_kernel/pallas_call | solution.py:671
  31.2 6.5 %collective-permute-done = bf16[64,3840]{1,0:T(8,128)(2,1)} collective-permute-done((bf16[64,3840]{1,0:T(8,128)(2,1)}, bf16[64,3840]{1,0:T(8,128)(2,1)}, u32[]{:S(2)}, u32[]{:S(2)}) %collective-permute-start) | collective-permute-done | bytes 491552 | tf_op jit(solution)/shard_map/ppermute | solution.py:743
  61.0 8.0 %decoder_front_kernel.1 = (f32[320,512]{1,0:T(8,128)S(1)}, bf16[176,512]{1,0:T(8,128)(2,1)S(1)}, bf16[320,512]{1,0:T(8,128)(2,1)S(1)}, bf16[320,512]{1,0:T(8,128...) custom-call(s32[18]{0:T(128)S(1)} %stack.111.sc_ref, ...), custom_call_target="tpu_custom_call" | custom-call | flops 8000000 | bytes 1 | tf_op jit(solution)/shard_map/decoder_front_kernel/pallas_call | solution.py:671
  69.0 5.4 %collective-permute-done.9 = bf16[64,4352]{1,0:T(8,128)(2,1)S(1)} collective-permute-done((bf16[64,4352]{1,0:T(8,128)(2,1)}, bf16[64,4352]{1,0:T(8,128)(2,1)S(1)}, u32[]{:S(2)}, u32[]{:S(2)}) %collective-permute-start.9) | collective-permute-done | bytes 557088 | tf_op jit(solution)/shard_map/ppermute | solution.py:743
  79.9 13.3 %decoder_layer_kernel.1 = (bf16[320,512]{1,0:T(8,128)(2,1)}, bf16[320,512]{1,0:T(8,128)(2,1)S(1)}, bf16[320,2048]{1,0:T(8,128)(2,1)S(1)}, f32[320,512]{1,0:T(8,1...) custom-call(s32[18]{0:T(128)S(1)} %stack.111.sc_ref, ...), custom_call_target="tpu_custom_call" | custom-call | flops 14000000 | bytes 1 | tf_op jit(solution)/shard_map/decoder_layer_kernel/pallas_call | solution.py:671
  95.0 3.2 %decoder_gradients_kernel.1 = (bf16[256,4608]{1,0:T(8,128)(2,1)S(1)}, bf16[256,4608]{1,0:T(8,128)(2,1)S(1)}) custom-call(s32[18]{0:T(128)S(1)} %stack.111.sc_ref, bf16[320,512]{1,0:T(8,128)(2,1)S(1)} %get-tuple-element.230.n2_ref, bf16[320,2048]{1,0:T(8,128)(2,1)S(1)} %get-tuple-element.231.active_ref, bf16[320,2048]{1,0:T(8,128)(2,1)S(1)} %get-tuple-element.232.dh_ref, ...), custom_call_target="tpu_custom_call" | custom-call | flops 5000000 | bytes 1 | tf_op jit(solution)/shard_map/decoder_gradients_kernel/pallas_call | solution.py:671
  101.0 2.5 collective-permute-start.20
  103.7 3.3 %decoder_back_kernel.1 = (bf16[320,512]{1,0:T(8,128)(2,1)S(1)}, bf16[320,1536]{1,0:T(8,128)(2,1)S(1)}, f32[8,512]{1,0:T(8,128)S(1)}) custom-call(s32[18]{0:T(128)S(1)} %stack.111.sc_ref, bf16[128,3840]{1,0:T(8,128)(2,1)S(1)} %pad_maximum_fusion.5.refs_0_, bf16[128,3840]{1,0:T(8,128)(2,1)S(1)} %pad_maximum_fusion.6.refs_1_, bf16[128,3840]{1,0:T(8,128)(2,1)S(1)} %copy-done.1, ...), custom_call_target="tpu_custom_call" | custom-call | flops 4000000 | bytes 1 | tf_op jit(solution)/shard_map/decoder_back_kernel/pallas_call | solution.py:671
  106.9 11.6 %collective-permute-done.20 = bf16[8,160,256]{2,1,0:T(8,128)(2,1)S(1)} collective-permute-done((bf16[8,160,256]{2,1,0:T(8,128)(2,1)S(1)}, bf16[8,160,256]{2,1,0:T(8,128)(2,1)S(1)}, u32[]{:S(2)}, u32[]{:S(2)}) %collective-permute-start.20) | collective-permute-done | bytes 655392 | tf_op jit(solution)/shard_map/ppermute | solution.py:698
  122.5 5.6 %encoder_front_kernel.1 = (bf16[320,512]{1,0:T(8,128)(2,1)S(1)}, bf16[336,512]{1,0:T(8,128)(2,1)S(1)}, bf16[576,512]{1,0:T(8,128)(2,1)S(1)}, bf16[576,512]{1,0:T(8,128)(2,1)S(1)}, bf16[336,512]{1,0:T(8,128)(2,1)S(1)}) custom-call(s32[18]{0:T(128)S(1)} %stack.111.sc_ref, bf16[128,4352]{1,0:T(8,128)(2,1)S(1)} %constant_dynamic-update-slice_fusion.3.refs_0_.refs_4_, ...), custom_call_target="tpu_custom_call" | custom-call | flops 7000000 | bytes 1 | tf_op jit(solution)/shard_map/encoder_front_kernel/pallas_call | solution.py:671
  128.2 5.2 %middle_kernel.1 = (f32[320,512]{1,0:T(8,128)S(1)}, bf16[160,512]{1,0:T(8,128)(2,1)S(1)}, bf16[160,256]{1,0:T(8,128)(2,1)S(1)}, f32[8,512]{1,0:T(8,128)S(1)}, bf...) custom-call(s32[18]{0:T(128)S(1)} %stack.111.sc_ref, bf16[128,3840]{1,0:T(8,128)(2,1)S(1)} %pad_maximum_fusion.5.refs_0_, ...), custom_call_target="tpu_custom_call" | custom-call | flops 7000000 | bytes 1 | tf_op jit(solution)/shard_map/middle_kernel/pallas_call | solution.py:671
  134.6 5.7 %encoder_forward_kernel.1 = (bf16[336,512]{1,0:T(8,128)(2,1)S(1)}, bf16[320,512]{1,0:T(8,128)(2,1)S(1)}, bf16[320,2048]{1,0:T(8,128)(2,1)S(1)}, f32[320,2048]{1,...) custom-call(s32[18]{0:T(128)S(1)} %stack.111.sc_ref, ...), custom_call_target="tpu_custom_call" | custom-call | flops 6000000 | bytes 1 | tf_op jit(solution)/shard_map/encoder_forward_kernel/pallas_call | solution.py:671
  140.3 7.5 %collective-permute-done.25 = bf16[128,4608]{1,0:T(8,128)(2,1)S(1)} collective-permute-done((bf16[128,4608]{1,0:T(8,128)(2,1)S(1)}, bf16[128,4608]{1,0:T(8,128)(2,1)S(1)}, u32[]{:S(2)}, u32[]{:S(2)}) %collective-permute-start.25) | collective-permute-done | bytes 1179680 | tf_op jit(solution)/shard_map/ppermute | solution.py:698
  151.5 2.5 collective-permute-start.26
  154.3 8.3 %encoder_backward_kernel.1 = (f32[320,512]{1,0:T(8,128)S(1)}, bf16[320,2048]{1,0:T(8,128)(2,1)S(1)}, bf16[320,512]{1,0:T(8,128)(2,1)S(1)}, bf16[320,512]{1,0:T(8...) custom-call(s32[18]{0:T(128)S(1)} %stack.111.sc_ref, ...), custom_call_target="tpu_custom_call" | custom-call | flops 11000000 | bytes 1 | tf_op jit(solution)/shard_map/encoder_backward_kernel/pallas_call | solution.py:671
  163.9 5.8 %collective-permute-done.26.x_ref = bf16[8,160,256]{2,1,0:T(8,128)(2,1)S(1)} collective-permute-done((bf16[8,160,256]{2,1,0:T(8,128)(2,1)S(1)}, bf16[8,160,256]{2,1,0:T(8,128)(2,1)S(1)}, u32[]{:S(2)}, u32[]{:S(2)}) %collective-permute-start.26) | collective-permute-done | bytes 655392 | tf_op jit(solution)/shard_map/ppermute | solution.py:743
  172.0 5.3 %collect_kernel.1 = (bf16[4,528,256]{2,1,0:T(8,128)(2,1)S(1)}, bf16[4,528,256]{2,1,0:T(8,128)(2,1)S(1)}) custom-call(s32[18]{0:T(128)S(1)} %stack.111.sc_ref, bf16[8,160,256]{2,1,0:T(8,128)(2,1)S(1)} %get-tuple-element.268.own_ref, bf16[8,160,256]{2,1,0:T(8,128)(2,1)S(1)} %collective-permute-done.26.x_ref, ...), custom_call_target="tpu_custom_call" | custom-call | flops 5000000 | bytes 1 | tf_op jit(solution)/shard_map/collect_kernel/pallas_call | solution.py:671
  177.3 3.9 %encoder_gradients_kernel.1 = (bf16[256,4096]{1,0:T(8,128)(2,1)S(1)}, bf16[256,4096]{1,0:T(8,128)(2,1)S(1)}, bf16[256,2816]{1,0:T(8,128)(2,1)S(1)}, bf16[256,2816]{1,0:T(8,128)(2,1)S(1)}) custom-call(s32[18]{0:T(128)S(1)} %stack.111.sc_ref, bf16[320,512]{1,0:T(8,128)(2,1)S(1)} %get-tuple-element.287.n2_ref, ...), custom_call_target="tpu_custom_call" | custom-call | flops 5000000 | bytes 1 | tf_op jit(solution)/shard_map/encoder_gradients_kernel/pallas_call | solution.py:671
  181.2 9.3 %collective-permute-start.32 = (bf16[256,2816]{1,0:T(8,128)(2,1)S(1)}, bf16[256,2816]{1,0:T(8,128)(2,1)S(1)}, u32[]{:S(2)}, u32[]{:S(2)}) collective-permute-start(bf16[256,2816]{1,0:T(8,128)(2,1)S(1)} %get-tuple-element.304), channel_id=1, source_target_pairs={{0,1},{1,0},{2,3},{3,2},{4,5},{5,4},{6,7},{7,6},{8,9},{9,8},{10,11... | collective-permute-start | bytes 4325384 | tf_op jit(solution)/shard_map/ppermute | solution.py:719
  193.6 2.6 collective-permute-done.31
  197.1 3.6 %encoder_back_kernel.1 = (bf16[320,512]{1,0:T(8,128)(2,1)}, bf16[256,1664]{1,0:T(8,128)(2,1)S(1)}, bf16[256,1664]{1,0:T(8,128)(2,1)S(1)}) custom-call(s32[18]{0:T(128)S(1)} %stack.111.sc_ref, bf16[128,4352]{1,0:T(8,128)(2,1)S(1)} %constant_dynamic-update-slice_fusion.3.refs_0_.refs_4_, bf16[128,4352]{1,0:T(8,128)(2,1)S(1)} %pad_maximum_fusion.1.refs_1_.refs_5_, ...), custom_call_target="tpu_custom_call" | custom-call | flops 5000000 | bytes 1 | tf_op jit(solution)/shard_map/encoder_back_kernel/pallas_call | solution.py:671
  207.4 7.9 %collective-permute-done.36 = bf16[64,3840]{1,0:T(8,128)(2,1)S(1)} collective-permute-done((bf16[64,3840]{1,0:T(8,128)(2,1)S(1)}, bf16[64,3840]{1,0:T(8,128)(2,1)S(1)}, u32[]{:S(2)}, u32[]{:S(2)}) %collective-permute-start.36) | collective-permute-done | bytes 491552 | tf_op jit(solution)/shard_map/ppermute | solution.py:698
  220.3 2.6 collective-permute-start.44
  224.2 5.0 %all-to-all-start.1 = ((bf16[4,16,8448]{2,1,0:T(8,128)(2,1)}), bf16[4,16,8448]{2,1,0:T(8,128)(2,1)S(1)}, u32[]{:S(2)}, u32[]{:S(2)}) async-start(bf16[4,16,8448]{2,1,0:T(8,128)(2,1)} %bitcast.207), calls=%async_computation.1 | async-start | bytes 2162688 | tf_op jit(solution)/shard_map/all_to_all | solution.py:726
  230.3 6.8 %collective-permute-done.34 = bf16[128,4096]{1,0:T(8,128)(2,1)} collective-permute-done((bf16[128,4096]{1,0:T(8,128)(2,1)}, bf16[128,4096]{1,0:T(8,128)(2,1)}, u32[]{:S(2)}, u32[]{:S(2)}) %collective-permute-start.34) | collective-permute-done | bytes 1048608 | tf_op jit(solution)/shard_map/ppermute | solution.py:698
  242.5 5.9 %collective-permute-done.44 = bf16[528,256]{1,0:T(8,128)(2,1)} collective-permute-done((bf16[528,256]{1,0:T(8,128)(2,1)}, bf16[528,256]{1,0:T(8,128)(2,1)}, u32[]{:S(2)}, u32[]{:S(2)}) %collective-permute-start.44) | collective-permute-done | bytes 270368 | tf_op jit(solution)/shard_map/ppermute | solution.py:711
  251.3 4.5 %collective-permute-done.41 = bf16[64,1664]{1,0:T(8,128)(2,1)S(1)} collective-permute-done((bf16[64,1664]{1,0:T(8,128)(2,1)S(1)}, bf16[64,1664]{1,0:T(8,128)(2,1)S(1)}, u32[]{:S(2)}, u32[]{:S(2)}) %collective-permute-start.41) | collective-permute-done | bytes 213024 | tf_op jit(solution)/shard_map/ppermute | solution.py:698
  255.9 3.4 %collective-permute-done.38 = bf16[64,4096]{1,0:T(8,128)(2,1)S(1)} collective-permute-done((bf16[64,4096]{1,0:T(8,128)(2,1)S(1)}, bf16[64,4096]{1,0:T(8,128)(2,1)S(1)}, u32[]{:S(2)}, u32[]{:S(2)}) %collective-permute-start.38) | collective-permute-done | bytes 524320 | tf_op jit(solution)/shard_map/ppermute | solution.py:698
  260.5 8.9 %all-to-all-done.1 = bf16[4,16,8448]{2,1,0:T(8,128)(2,1)S(1)} async-done(((bf16[4,16,8448]{2,1,0:T(8,128)(2,1)}), bf16[4,16,8448]{2,1,0:T(8,128)(2,1)S(1)}, u32[]{:S(2)}, u32[]{:S(2)}) %all-to-all-start.1) | async-done | bytes 1081376 | tf_op jit(solution)/shard_map/all_to_all | solution.py:726
  270.5 3.8 %all-to-all-start = ((bf16[4,16,8576]{2,1,0:T(8,128)(2,1)}), bf16[4,16,8576]{2,1,0:T(8,128)(2,1)S(1)}, u32[]{:S(2)}, u32[]{:S(2)}) async-start(bf16[4,16,8576]{2,1,0:T(8,128)(2,1)} %bitcast.87), calls=%async_computation | async-start | bytes 2195456 | tf_op jit(solution)/shard_map/all_to_all | solution.py:726
  279.5 19.8 %all-to-all-done = bf16[4,16,8576]{2,1,0:T(8,128)(2,1)S(1)} async-done(((bf16[4,16,8576]{2,1,0:T(8,128)(2,1)}), bf16[4,16,8576]{2,1,0:T(8,128)(2,1)S(1)}, u32[]{:S(2)}, u32[]{:S(2)}) %all-to-all-start) | async-done | bytes 1097760 | tf_op jit(solution)/shard_map/all_to_all | solution.py:726
  (303 shorter events, 105.0 us)
Async XLA Ops:
  23.4 14.4 %collective-permute-start = (bf16[64,3840]{1,0:T(8,128)(2,1)}, bf16[64,3840]{1,0:T(8,128)(2,1)}, u32[]{:S(2)}, u32[]{:S(2)}) collective-permute-start(bf16[64,3840]{1,0:T(8,128)(2,1)} %constant_dynamic-slice_fusion.5), channel_id=1, source_target_pairs={{0,2},{2,0},{1,3},{3,1},{4,6},{6,4},{5,7},{7,5},{8,10},{10,8},{9,1... | collective-permute-start | bytes 1474568 | tf_op jit(solution)/shard_map/ppermute | solution.py:743
  31.1 25.6 %collective-permute-start.4 = (f32[304,256]{1,0:T(8,128)}, f32[304,256]{1,0:T(8,128)}, u32[]{:S(2)}, u32[]{:S(2)}) collective-permute-start(f32[304,256]{1,0:T(8,128)} %dynamic-slice_bitcast_fusion.10), channel_id=1, source_target_pairs={{0,2},{2,0},{1,3},{3,1},{4,6},{6,4},{5,7},{7,5},{8,10},{10,8},{9,1... | collective-permute-start | bytes 933896 | tf_op jit(solution)/shard_map/ppermute | solution.py:743
  43.7 14.0 %collective-permute-start.5 = (bf16[64,4608]{1,0:T(8,128)(2,1)}, bf16[64,4608]{1,0:T(8,128)(2,1)}, u32[]{:S(2)}, u32[]{:S(2)}) collective-permute-start(bf16[64,4608]{1,0:T(8,128)(2,1)} %constant_dynamic-slice_fusion.4), channel_id=1, source_target_pairs={{0,2},{2,0},{1,3},{3,1},{4,6},{6,4},{5,7},{7,5},{8,10},{10,8},{9,1... | collective-permute-start | bytes 1769480 | tf_op jit(solution)/shard_map/ppermute | solution.py:743
  57.7 16.6 %collective-permute-start.8 = (bf16[64,4608]{1,0:T(8,128)(2,1)}, bf16[64,4608]{1,0:T(8,128)(2,1)S(1)}, u32[]{:S(2)}, u32[]{:S(2)}) collective-permute-start(bf16[64,4608]{1,0:T(8,128)(2,1)} %collective-permute-done.5), channel_id=1, source_target_pairs={{0,4},{4,0},{1,5},{5,1},{2,6},{6,2},{3,7},{7,3},{8,12},{12,8},{9,1... | collective-permute-start | bytes 1769480 | tf_op jit(solution)/shard_map/ppermute | solution.py:743
  59.4 14.9 %collective-permute-start.9 = (bf16[64,4352]{1,0:T(8,128)(2,1)}, bf16[64,4352]{1,0:T(8,128)(2,1)S(1)}, u32[]{:S(2)}, u32[]{:S(2)}) collective-permute-start(bf16[64,4352]{1,0:T(8,128)(2,1)} %constant_dynamic-slice_fusion.3), channel_id=1, source_target_pairs={{0,2},{2,0},{1,3},{3,1},{4,6},{6,4},{5,7},{7,5},{8,10},{10,8},{9,1... | collective-permute-start | bytes 1671176 | tf_op jit(solution)/shard_map/ppermute | solution.py:743
  60.9 19.0 %collective-permute-start.10 = (bf16[128,4608]{1,0:T(8,128)(2,1)S(1)}, bf16[128,4608]{1,0:T(8,128)(2,1)S(1)}, u32[]{:S(2)}, u32[]{:S(2)}) collective-permute-start(bf16[128,4608]{1,0:T(8,128)(2,1)S(1)} %copy-done.6), channel_id=1, source_target_pairs={{0,1},{1,0},{2,3},{3,2},{4,5},{5,4},{6,7},{7,6},{8,9},{9,8},{10,11... | collective-permute-start | bytes 3538952 | tf_op jit(solution)/shard_map/ppermute | solution.py:743
  74.3 20.2 %collective-permute-start.14 = (bf16[2,8,160,256]{3,2,1,0:T(8,128)(2,1)S(1)}, bf16[2,8,160,256]{3,2,1,0:T(8,128)(2,1)S(1)}, u32[]{:S(2)}, u32[]{:S(2)}) collective-permute-start(bf16[2,8,160,256]{3,2,1,0:T(8,128)(2,1)S(1)} %copy-done.16), channel_id=1, source_target_pairs={{0,1},{1,0},{2,3},{3,2},{4,5},{5,4},{6,7},{7,6},{8,9},{9,8},{10,11... | collective-permute-start | bytes 3932168 | tf_op jit(solution)/shard_map/ppermute | solution.py:719
  77.2 17.8 %collective-permute-start.12 = (bf16[64,4352]{1,0:T(8,128)(2,1)S(1)}, bf16[64,4352]{1,0:T(8,128)(2,1)S(1)}, u32[]{:S(2)}, u32[]{:S(2)}) collective-permute-start(bf16[64,4352]{1,0:T(8,128)(2,1)S(1)} %collective-permute-done.9), channel_id=1, source_target_pairs={{0,4},{4,0},{1,5},{5,1},{2,6},{6,2},{3,7},{7,3},{8,12},{12,8},{9,1... | collective-permute-start | bytes 1671176 | tf_op jit(solution)/shard_map/ppermute | solution.py:743
  78.4 16.6 %collective-permute-start.13 = (bf16[64,4096]{1,0:T(8,128)(2,1)S(1)}, bf16[64,4096]{1,0:T(8,128)(2,1)S(1)}, u32[]{:S(2)}, u32[]{:S(2)}) collective-permute-start(bf16[64,4096]{1,0:T(8,128)(2,1)S(1)} %constant_dynamic-slice_fusion), channel_id=1, source_target_pairs={{0,2},{2,0},{1,3},{3,1},{4,6},{6,4},{5,7},{7,5},{8,10},{10,8},{9,1... | collective-permute-start | bytes 1572872 | tf_op jit(solution)/shard_map/ppermute | solution.py:743
  98.2 20.9 %collective-permute-start.17 = (bf16[256,4608]{1,0:T(8,128)(2,1)S(1)}, bf16[256,4608]{1,0:T(8,128)(2,1)S(1)}, u32[]{:S(2)}, u32[]{:S(2)}) collective-permute-start(bf16[256,4608]{1,0:T(8,128)(2,1)S(1)} %get-tuple-element.238), channel_id=1, source_target_pairs={{0,1},{1,0},{2,3},{3,2},{4,5},{5,4},{6,7},{7,6},{8,9},{9,8},{10,11... | collective-permute-start | bytes 7077896 | tf_op jit(solution)/shard_map/ppermute | solution.py:719
  99.4 21.8 %collective-permute-start.15 = (bf16[128,4352]{1,0:T(8,128)(2,1)S(1)}, bf16[128,4352]{1,0:T(8,128)(2,1)S(1)}, u32[]{:S(2)}, u32[]{:S(2)}) collective-permute-start(bf16[128,4352]{1,0:T(8,128)(2,1)S(1)} %constant_dynamic-update-slice_fusion.3.refs_0_.refs_4_), channel_id=1, source_target_pairs={{0,1},{1,0},{2,3},{3,2},{4,5},{5,4},{6,7},{7,6},{8,9},{9,8},{10,11... | collective-permute-start | bytes 3342344 | tf_op jit(solution)/shard_map/ppermute | solution.py:743
  99.5 35.1 %collective-permute-start.21 = (bf16[128,4096]{1,0:T(8,128)(2,1)S(1)}, bf16[128,4096]{1,0:T(8,128)(2,1)S(1)}, u32[]{:S(2)}, u32[]{:S(2)}) collective-permute-start(bf16[128,4096]{1,0:T(8,128)(2,1)S(1)} %constant_dynamic-update-slice_fusion.7.refs_4_), channel_id=1, source_target_pairs={{0,1},{1,0},{2,3},{3,2},{4,5},{5,4},{6,7},{7,6},{8,9},{9,8},{10,11... | collective-permute-start | bytes 3145736 | tf_op jit(solution)/shard_map/ppermute | solution.py:743
  99.9 19.8 %collective-permute-start.19 = (bf16[64,4096]{1,0:T(8,128)(2,1)S(1)}, bf16[64,4096]{1,0:T(8,128)(2,1)S(1)}, u32[]{:S(2)}, u32[]{:S(2)}) collective-permute-start(bf16[64,4096]{1,0:T(8,128)(2,1)S(1)} %collective-permute-done.13), channel_id=1, source_target_pairs={{0,4},{4,0},{1,5},{5,1},{2,6},{6,2},{3,7},{7,3},{8,12},{12,8},{9,1... | collective-permute-start | bytes 1572872 | tf_op jit(solution)/shard_map/ppermute | solution.py:743
  101.0 17.5 %collective-permute-start.20 = (bf16[8,160,256]{2,1,0:T(8,128)(2,1)S(1)}, bf16[8,160,256]{2,1,0:T(8,128)(2,1)S(1)}, u32[]{:S(2)}, u32[]{:S(2)}) collective-permute-start(bf16[8,160,256]{2,1,0:T(8,128)(2,1)S(1)} %dynamic-slice_bitcast_fusion.4), channel_id=1, source_target_pairs={{0,2},{2,0},{1,3},{3,1},{4,6},{6,4},{5,7},{7,5},{8,10},{10,8},{9,1... | collective-permute-start | bytes 1966088 | tf_op jit(solution)/shard_map/ppermute | solution.py:698
  119.8 28.1 %collective-permute-start.25 = (bf16[128,4608]{1,0:T(8,128)(2,1)S(1)}, bf16[128,4608]{1,0:T(8,128)(2,1)S(1)}, u32[]{:S(2)}, u32[]{:S(2)}) collective-permute-start(bf16[128,4608]{1,0:T(8,128)(2,1)S(1)} %dynamic-slice_bitcast_fusion), channel_id=1, source_target_pairs={{0,4},{4,0},{1,5},{5,1},{2,6},{6,2},{3,7},{7,3},{8,12},{12,8},{9,1... | collective-permute-start | bytes 3538952 | tf_op jit(solution)/shard_map/ppermute | solution.py:698
  121.1 13.5 %collective-permute-start.22 = (bf16[128,4096]{1,0:T(8,128)(2,1)S(1)}, bf16[128,4096]{1,0:T(8,128)(2,1)S(1)}, u32[]{:S(2)}, u32[]{:S(2)}) collective-permute-start(bf16[128,4096]{1,0:T(8,128)(2,1)S(1)} %pad_maximum_fusion.4.refs_5_), channel_id=1, source_target_pairs={{0,1},{1,0},{2,3},{3,2},{4,5},{5,4},{6,7},{7,6},{8,9},{9,8},{10,11... | collective-permute-start | bytes 3145736 | tf_op jit(solution)/shard_map/ppermute | solution.py:743
  133.4 14.8 %collective-permute-start.24 = (bf16[256,3840]{1,0:T(8,128)(2,1)S(1)}, bf16[256,3840]{1,0:T(8,128)(2,1)S(1)}, u32[]{:S(2)}, u32[]{:S(2)}) collective-permute-start(bf16[256,3840]{1,0:T(8,128)(2,1)S(1)} %get-tuple-element.263), channel_id=1, source_target_pairs={{0,1},{1,0},{2,3},{3,2},{4,5},{5,4},{6,7},{7,6},{8,9},{9,8},{10,11... | collective-permute-start | bytes 5898248 | tf_op jit(solution)/shard_map/ppermute | solution.py:719
  148.7 23.0 %collective-permute-start.29 = (bf16[128,3840]{1,0:T(8,128)(2,1)S(1)}, bf16[128,3840]{1,0:T(8,128)(2,1)S(1)}, u32[]{:S(2)}, u32[]{:S(2)}) collective-permute-start(bf16[128,3840]{1,0:T(8,128)(2,1)S(1)} %dynamic-slice_bitcast_fusion.2), channel_id=1, source_target_pairs={{0,4},{4,0},{1,5},{5,1},{2,6},{6,2},{3,7},{7,3},{8,12},{12,8},{9,1... | collective-permute-start | bytes 2949128 | tf_op jit(solution)/shard_map/ppermute | solution.py:698
  151.5 18.2 %collective-permute-start.26 = (bf16[8,160,256]{2,1,0:T(8,128)(2,1)S(1)}, bf16[8,160,256]{2,1,0:T(8,128)(2,1)S(1)}, u32[]{:S(2)}, u32[]{:S(2)}) collective-permute-start(bf16[8,160,256]{2,1,0:T(8,128)(2,1)S(1)} %get-tuple-element.268.own_ref), channel_id=1, source_target_pairs={{0,2},{2,0},{1,3},{3,1},{4,6},{6,4},{5,7},{7,5},{8,10},{10,8},{9,1... | collective-permute-start | bytes 1966088 | tf_op jit(solution)/shard_map/ppermute | solution.py:743
  154.1 15.6 %collective-permute-start.27 = (bf16[8,160,256]{2,1,0:T(8,128)(2,1)S(1)}, bf16[8,160,256]{2,1,0:T(8,128)(2,1)S(1)}, u32[]{:S(2)}, u32[]{:S(2)}) collective-permute-start(bf16[8,160,256]{2,1,0:T(8,128)(2,1)S(1)} %get-tuple-element.268.own_ref), channel_id=1, source_target_pairs={{0,1},{1,0},{2,3},{3,2},{4,5},{5,4},{6,7},{7,6},{8,9},{9,8},{10,11... | collective-permute-start | bytes 1966088 | tf_op jit(solution)/shard_map/ppermute | solution.py:743
  154.1 36.4 %collective-permute-start.33 = (bf16[64,4608]{1,0:T(8,128)(2,1)S(1)}, bf16[64,4608]{1,0:T(8,128)(2,1)S(1)}, u32[]{:S(2)}, u32[]{:S(2)}) collective-permute-start(bf16[64,4608]{1,0:T(8,128)(2,1)S(1)} %dynamic-slice_bitcast_fusion.5), channel_id=1, source_target_pairs={{0,2},{2,0},{1,3},{3,1},{4,6},{6,4},{5,7},{7,5},{8,10},{10,8},{9,1... | collective-permute-start | bytes 1769480 | tf_op jit(solution)/shard_map/ppermute | solution.py:698
  162.6 14.7 %collective-permute-start.30 = (bf16[256,1024]{1,0:T(8,128)(2,1)S(1)}, bf16[256,1024]{1,0:T(8,128)(2,1)S(1)}, u32[]{:S(2)}, u32[]{:S(2)}) collective-permute-start(bf16[256,1024]{1,0:T(8,128)(2,1)S(1)} %get-tuple-element.286), channel_id=1, source_target_pairs={{1,0},{2,1},{3,2},{5,4},{6,5},{7,6},{9,8},{10,9},{11,10},{13,12},{... | collective-permute-start | bytes 1572872 | tf_op jit(solution)/shard_map/ppermute | solution.py:733
  190.6 26.7 %collective-permute-start.35 = (bf16[4,528,256]{2,1,0:T(8,128)(2,1)S(1)}, bf16[4,528,256]{2,1,0:T(8,128)(2,1)S(1)}, u32[]{:S(2)}, u32[]{:S(2)}) collective-permute-start(bf16[4,528,256]{2,1,0:T(8,128)(2,1)S(1)} %get-tuple-element.320), channel_id=1, source_target_pairs={{0,4},{4,0},{1,5},{5,1},{2,6},{6,2},{3,7},{7,3},{8,12},{12,8},{9,1... | collective-permute-start | bytes 3244040 | tf_op jit(solution)/shard_map/ppermute | solution.py:719
  201.1 14.1 %collective-permute-start.36 = (bf16[64,3840]{1,0:T(8,128)(2,1)S(1)}, bf16[64,3840]{1,0:T(8,128)(2,1)S(1)}, u32[]{:S(2)}, u32[]{:S(2)}) collective-permute-start(bf16[64,3840]{1,0:T(8,128)(2,1)S(1)} %dynamic-slice_bitcast_fusion.7), channel_id=1, source_target_pairs={{0,2},{2,0},{1,3},{3,1},{4,6},{6,4},{5,7},{7,5},{8,10},{10,8},{9,1... | collective-permute-start | bytes 1474568 | tf_op jit(solution)/shard_map/ppermute | solution.py:698
  202.4 34.7 %collective-permute-start.34 = (bf16[128,4096]{1,0:T(8,128)(2,1)}, bf16[128,4096]{1,0:T(8,128)(2,1)}, u32[]{:S(2)}, u32[]{:S(2)}) collective-permute-start(bf16[128,4096]{1,0:T(8,128)(2,1)} %dynamic-slice_bitcast_fusion.1), channel_id=1, source_target_pairs={{0,2},{2,0},{1,3},{3,1},{4,6},{6,4},{5,7},{7,5},{8,10},{10,8},{9,1... | collective-permute-start | bytes 3145736 | tf_op jit(solution)/shard_map/ppermute | solution.py:698
  205.3 34.3 %collective-permute-start.40 = (bf16[128,2816]{1,0:T(8,128)(2,1)}, bf16[128,2816]{1,0:T(8,128)(2,1)}, u32[]{:S(2)}, u32[]{:S(2)}) collective-permute-start(bf16[128,2816]{1,0:T(8,128)(2,1)} %dynamic-slice_bitcast_fusion.3), channel_id=1, source_target_pairs={{0,4},{4,0},{1,5},{5,1},{2,6},{6,2},{3,7},{7,3},{8,12},{12,8},{9,1... | collective-permute-start | bytes 2162696 | tf_op jit(solution)/shard_map/ppermute | solution.py:698
  218.7 22.6 %collective-permute-start.43 = (bf16[528,256]{1,0:T(8,128)(2,1)}, bf16[528,256]{1,0:T(8,128)(2,1)}, u32[]{:S(2)}, u32[]{:S(2)}) collective-permute-start(bf16[528,256]{1,0:T(8,128)(2,1)} %get-tuple-element.359), channel_id=1, source_target_pairs={{0,8},{8,0},{16,24},{24,16},{1,9},{9,1},{17,25},{25,17},{2,10},{10... | collective-permute-start | bytes 811016 | tf_op jit(solution)/shard_map/ppermute | solution.py:711
  220.3 28.1 %collective-permute-start.44 = (bf16[528,256]{1,0:T(8,128)(2,1)}, bf16[528,256]{1,0:T(8,128)(2,1)}, u32[]{:S(2)}, u32[]{:S(2)}) collective-permute-start(bf16[528,256]{1,0:T(8,128)(2,1)} %get-tuple-element.361), channel_id=1, source_target_pairs={{0,16},{8,24},{16,0},{24,8},{1,17},{9,25},{17,1},{25,9},{2,18},{10... | collective-permute-start | bytes 811016 | tf_op jit(solution)/shard_map/ppermute | solution.py:711
  222.9 25.5 %collective-permute-start.45 = (bf16[528,256]{1,0:T(8,128)(2,1)}, bf16[528,256]{1,0:T(8,128)(2,1)}, u32[]{:S(2)}, u32[]{:S(2)}) collective-permute-start(bf16[528,256]{1,0:T(8,128)(2,1)} %get-tuple-element.360), channel_id=1, source_target_pairs={{0,24},{8,16},{16,8},{24,0},{1,25},{9,17},{17,9},{25,1},{2,26},{10... | collective-permute-start | bytes 811016 | tf_op jit(solution)/shard_map/ppermute | solution.py:711
  224.2 45.3 %all-to-all-start.1 = ((bf16[4,16,8448]{2,1,0:T(8,128)(2,1)}), bf16[4,16,8448]{2,1,0:T(8,128)(2,1)S(1)}, u32[]{:S(2)}, u32[]{:S(2)}) async-start(bf16[4,16,8448]{2,1,0:T(8,128)(2,1)} %bitcast.207), calls=%async_computation.1 | async-start | bytes 2162688 | tf_op jit(solution)/shard_map/all_to_all | solution.py:726
  241.3 18.0 %collective-permute-start.38 = (bf16[64,4096]{1,0:T(8,128)(2,1)S(1)}, bf16[64,4096]{1,0:T(8,128)(2,1)S(1)}, u32[]{:S(2)}, u32[]{:S(2)}) collective-permute-start(bf16[64,4096]{1,0:T(8,128)(2,1)S(1)} %dynamic-slice_bitcast_fusion.6), channel_id=1, source_target_pairs={{0,4},{4,0},{1,5},{5,1},{2,6},{6,2},{3,7},{7,3},{8,12},{12,8},{9,1... | collective-permute-start | bytes 1572872 | tf_op jit(solution)/shard_map/ppermute | solution.py:698
  270.5 28.9 %all-to-all-start = ((bf16[4,16,8576]{2,1,0:T(8,128)(2,1)}), bf16[4,16,8576]{2,1,0:T(8,128)(2,1)S(1)}, u32[]{:S(2)}, u32[]{:S(2)}) async-start(bf16[4,16,8576]{2,1,0:T(8,128)(2,1)} %bitcast.87), calls=%async_computation | async-start | bytes 2195456 | tf_op jit(solution)/shard_map/all_to_all | solution.py:726
  (72 other events, 438.8 us)
